TPU v7x, 32 devices: a whole 2x2x4 slice. The times are simulated.
32 devices in a mesh: wide: 8 (over z, x), narrow: 4 (over y, core).
Axes of the slice: x: 2, y: 2, z: 4, core: 2. Of those that a mesh axis runs over, the one named last changes fastest.
Arguments:
- hidden_in: bfloat16 [512, 2048], P(('wide', 'narrow')), may hold values from -6 to 6
- queries: bfloat16 [512, 2048], P(('wide', 'narrow')), may hold values from -6 to 6
- cache_key: bfloat16 [512, 128, 256], P(('wide', 'narrow')), may hold values from -6 to 6
- cache_value: bfloat16 [512, 128, 256], P(('wide', 'narrow')), may hold values from -6 to 6
- new_key: bfloat16 [512, 256], P(('wide', 'narrow')), may hold values from -6 to 6
- new_value: bfloat16 [512, 256], P(('wide', 'narrow')), may hold values from -6 to 6
- lengths: int32 [512], P(('wide', 'narrow')), may hold values from 2 to 128, as said below
- norm_gain: bfloat16 [2048], replicated, may hold values from 0.5 to 1.5
- gate_codes: bfloat16 [32, 2048, 384], P(('wide', 'narrow')), may hold values from -4 to 4
- gate_scale: float32 [32, 16, 3], P(('wide', 'narrow')), may hold values from 0.011048543 to 0.044194173
- up_codes: bfloat16 [32, 2048, 384], P(('wide', 'narrow')), may hold values from -4 to 4
- up_scale: float32 [32, 16, 3], P(('wide', 'narrow')), may hold values from 0.011048543 to 0.044194173
- down_codes: bfloat16 [32, 384, 2048], P(('wide', 'narrow')), may hold values from -4 to 4
- down_scale: float32 [32, 3, 16], P(('wide', 'narrow')), may hold values from 0.018042196 to 0.07216878
- think_ids: int32 [512, 8], P(('wide', 'narrow')), may hold values from 0 to 15, all different within a row; in each aligned block of 16 rows (0 to 15, 16 to 31, ...) at most 16 rows name the same one
- think_gates: float32 [512, 8], P(('wide', 'narrow')), may hold values from 0.05 to 0.3
- talker_source: int32 [512], P(('wide', 'narrow')), may hold values from 0 to 511, as said below
- talker_gain: bfloat16 [2048], replicated, may hold values from 0.5 to 1.5
- talk_gate_w: bfloat16 [4, 2048, 384], P('narrow'), may hold values from -0.125 to 0.125
- talk_up_w: bfloat16 [4, 2048, 384], P('narrow'), may hold values from -0.125 to 0.125
- talk_down_w: bfloat16 [4, 384, 1024], P('narrow'), may hold values from -0.3125 to 0.3125
- talk_ids: int32 [512, 2], P(('wide', 'narrow')), may hold values from 0 to 3, all different within a row; in each aligned block of 16 rows (0 to 15, 16 to 31, ...) at most 16 rows name the same one
- talk_gates: float32 [512, 2], P(('wide', 'narrow')), may hold values from 0.3 to 0.7
Outputs:
- thinker_out: bfloat16 [512, 2048], P(('wide', 'narrow'))
- talker_out: bfloat16 [512, 1024], P(('wide', 'narrow'))
Inputs may be any that keep to these rules, and one draw needn't show every extreme that they name: `think_ids`: each row names 8 different thinker experts; among the rows of one device no expert is named by more than 16 rows. `talk_ids`: each position names 2 different talker experts; among the positions of one device no expert is named by more than 16. `lengths`: some row uses all 128 cached positions. `talker_source`: A permutation of the rows. The row feeding a talker position lies on the same narrow index as the position. The rows of one device feed positions on exactly 8 devices, 2 positions on each.
All inputs are finite; a program needn't handle non-finite values.
Results may differ from a plain program's by a relative error of at most 0.018.
Values may be sent and summed in bfloat16 or wider, within the bound.
A program may use at most 64 MiB of HBM per device.

v0:
```python
import jax
import jax.numpy as jnp
from jax import lax
from jax.sharding import PartitionSpec as P

HEADS = 16
KV_HEADS = 2
HEAD_DIM = 128
BLK = 128
TOP = 8
TTOP = 2


EPSILON = 1e-06


def dequantize(code_block, scale_block):
    height, breadth = code_block.shape
    tiles = code_block.astype(jnp.float32).reshape(height // BLK, BLK, breadth // BLK, BLK)
    tiles = tiles * scale_block[:, None, :, None]
    return tiles.reshape(height, breadth).astype(jnp.bfloat16)


def rms_norm(values, gain):
    values = values.astype(jnp.float32)
    spread = jnp.mean(values * values, axis=-1, keepdims=True)
    return (values * lax.rsqrt(spread + EPSILON) * gain.astype(jnp.float32)).astype(jnp.bfloat16)


def swiglu(inputs, gate_dense, up_dense, down_dense):
    gated = jnp.dot(inputs, gate_dense, preferred_element_type=jnp.float32)
    lifted = jnp.dot(inputs, up_dense, preferred_element_type=jnp.float32)
    middle = (jax.nn.silu(gated) * lifted).astype(jnp.bfloat16)
    return jnp.dot(middle, down_dense, preferred_element_type=jnp.float32).astype(jnp.bfloat16)


def attend(queries, cache_key, cache_value, new_key, new_value, lengths):
    row_count = queries.shape[0]
    positions = cache_key.shape[1]
    groups = HEADS // KV_HEADS
    scaling = HEAD_DIM ** (-0.5)
    asked = queries.reshape(row_count, KV_HEADS, groups, HEAD_DIM)
    cached_keys = cache_key.reshape(row_count, positions, KV_HEADS, HEAD_DIM)
    cached_values = cache_value.reshape(row_count, positions, KV_HEADS, HEAD_DIM)
    scores = (
        jnp.einsum("rkgd,rtkd->rkgt", asked, cached_keys, preferred_element_type=jnp.float32)
        * scaling
    )
    newest_key = new_key.reshape(row_count, KV_HEADS, HEAD_DIM)
    fresh_score = (
        jnp.einsum("rkgd,rkd->rkg", asked, newest_key, preferred_element_type=jnp.float32) * scaling
    )
    places = jnp.arange(positions, dtype=jnp.int32)
    live_mask = places[None, :] < lengths[:, None]
    scores = jnp.where(live_mask[:, None, None, :], scores, -jnp.inf)
    highest = jnp.maximum(jnp.max(scores, axis=-1), fresh_score)
    weights = jnp.exp(scores - highest[..., None])
    own_weight = jnp.exp(fresh_score - highest)
    totals = jnp.sum(weights, axis=-1) + own_weight
    probabilities = (weights / totals[..., None]).astype(jnp.bfloat16)
    own_prob = (own_weight / totals).astype(jnp.bfloat16)
    mixture = jnp.einsum(
        "rkgt,rtkd->rkgd", probabilities, cached_values, preferred_element_type=jnp.float32
    )
    newest = new_value.reshape(row_count, KV_HEADS, 1, HEAD_DIM).astype(jnp.float32)
    mixture = mixture + own_prob.astype(jnp.float32)[..., None] * newest
    return mixture.reshape(row_count, HEADS * HEAD_DIM)


def slot_tables(expert_ids, gate_weights, expert_count, capacity):
    chosen = expert_ids[:, :, None] == jnp.arange(expert_count, dtype=jnp.int32)[None, None, :]
    picked = jnp.any(chosen, axis=1).astype(jnp.int32)
    weight_of = jnp.sum(jnp.where(chosen, gate_weights[:, :, None], jnp.float32(0.0)), axis=1)
    ranks = jnp.cumsum(picked, axis=0) - picked
    onehot = (picked[:, :, None] == 1) & (
        ranks[:, :, None] == jnp.arange(capacity, dtype=jnp.int32)[None, None, :]
    )
    placing = jnp.transpose(onehot, (1, 2, 0))
    return (placing, weight_of)


def local(
    hidden_in,
    queries,
    cache_key,
    cache_value,
    new_key,
    new_value,
    lengths,
    norm_gain,
    gate_codes,
    gate_scale,
    up_codes,
    up_scale,
    down_codes,
    down_scale,
    think_ids,
    think_gates,
    talker_source,
    talker_gain,
    talk_gate_w,
    talk_up_w,
    talk_down_w,
    talk_ids,
    talk_gates,
):
    wide_count = lax.axis_size("wide")
    narrow_count = lax.axis_size("narrow")
    row_count = hidden_in.shape[0]
    breadth = hidden_in.shape[1]
    attended = attend(queries, cache_key, cache_value, new_key, new_value, lengths)
    residual = hidden_in.astype(jnp.float32) + attended
    normed = rms_norm(residual, norm_gain)
    experts = wide_count * narrow_count // 2
    capacity = min(row_count, max(2, 2 * row_count * TOP // experts))
    placing, weight_of = slot_tables(think_ids, think_gates, experts, capacity)
    outgoing = jnp.einsum(
        "ecr,rd->ecd", placing.astype(jnp.bfloat16), normed, preferred_element_type=jnp.float32
    ).astype(jnp.bfloat16)
    doubled = jnp.broadcast_to(outgoing[:, None], (experts, 2, capacity, breadth)).reshape(
        wide_count, narrow_count, capacity, breadth
    )
    arrived = lax.all_to_all(
        lax.all_to_all(doubled, "wide", split_axis=0, concat_axis=0, tiled=True),
        "narrow",
        split_axis=1,
        concat_axis=1,
        tiled=True,
    )
    gate_dense = dequantize(gate_codes[0], gate_scale[0])
    up_dense = dequantize(up_codes[0], up_scale[0])
    down_dense = dequantize(down_codes[0], down_scale[0])
    produced = swiglu(arrived.reshape(-1, breadth), gate_dense, up_dense, down_dense)
    produced = produced.reshape(wide_count, narrow_count, capacity, breadth)
    returned = lax.all_to_all(
        lax.all_to_all(produced, "wide", split_axis=0, concat_axis=0, tiled=True),
        "narrow",
        split_axis=1,
        concat_axis=1,
        tiled=True,
    )
    paired = returned.reshape(experts, 2, capacity, breadth)
    summed = paired[:, 0].astype(jnp.float32) + paired[:, 1].astype(jnp.float32)
    combine = placing.astype(jnp.float32) * jnp.transpose(weight_of)[:, None, :]
    routed = jnp.einsum("ecr,ecd->rd", combine, summed, precision=lax.Precision.HIGHEST)
    thinker_out = (residual + routed).astype(jnp.bfloat16)
    own_wide = talker_source // row_count // narrow_count
    own_local = talker_source % row_count
    gathered = lax.all_gather(thinker_out, "wide", axis=0, tiled=True)
    talker_in = jnp.take(gathered, own_wide * row_count + own_local, axis=0)
    talker_normed = rms_norm(talker_in, talker_gain)
    talk_capacity = min(row_count, max(2, 2 * row_count * TTOP // narrow_count))
    talk_placing, talk_weight = slot_tables(talk_ids, talk_gates, narrow_count, talk_capacity)
    talk_outgoing = jnp.einsum(
        "ecr,rd->ecd",
        talk_placing.astype(jnp.bfloat16),
        talker_normed,
        preferred_element_type=jnp.float32,
    ).astype(jnp.bfloat16)
    incoming = lax.all_to_all(talk_outgoing, "narrow", split_axis=0, concat_axis=0, tiled=True)
    sources = incoming.shape[0]
    items = incoming.shape[1]
    result = swiglu(incoming.reshape(-1, breadth), talk_gate_w[0], talk_up_w[0], talk_down_w[0])
    talk_done = result.reshape(sources, items, -1)
    talk_back = lax.all_to_all(talk_done, "narrow", split_axis=0, concat_axis=0, tiled=True)
    talk_combine = talk_placing.astype(jnp.float32) * jnp.transpose(talk_weight)[:, None, :]
    talked = jnp.einsum(
        "ecr,ecd->rd", talk_combine, talk_back.astype(jnp.float32), precision=lax.Precision.HIGHEST
    )
    return (thinker_out, talked.astype(jnp.bfloat16))


def solution(mesh):
    return jax.shard_map(
        local,
        mesh=mesh,
        in_specs=(
            P(("wide", "narrow"), None),
            P(("wide", "narrow"), None),
            P(("wide", "narrow"), None, None),
            P(("wide", "narrow"), None, None),
            P(("wide", "narrow"), None),
            P(("wide", "narrow"), None),
            P(("wide", "narrow")),
            P(),
            P(("wide", "narrow"), None, None),
            P(("wide", "narrow"), None, None),
            P(("wide", "narrow"), None, None),
            P(("wide", "narrow"), None, None),
            P(("wide", "narrow"), None, None),
            P(("wide", "narrow"), None, None),
            P(("wide", "narrow"), None),
            P(("wide", "narrow"), None),
            P(("wide", "narrow")),
            P(),
            P("narrow", None, None),
            P("narrow", None, None),
            P("narrow", None, None),
            P(("wide", "narrow"), None),
            P(("wide", "narrow"), None),
        ),
        out_specs=(P(("wide", "narrow"), None), P(("wide", "narrow"), None)),
        check_vma=False,
    )
```

profile of v0, /device:TPU:0, one launch (start us, length us, event | category | flops | bytes accessed | tf_op | source)
XLA Modules:
  0.0 252.0 jit_solution(17728469713663613248)
XLA Ops:
  0.6 0.0 copy-start
  0.6 1.0 copy.123
  1.6 0.7 iota_compare_fusion.3
  2.3 0.7 reshape.215
  3.1 0.1 fusion.91
  3.2 0.0 copy-start.7
  3.2 0.0 copy-start.9
  3.2 2.0 fusion.90
  5.2 0.0 copy-start.10
  5.3 0.2 fusion.50
  5.5 0.7 reshape.195
  6.2 1.7 convolution_add_fusion
  7.9 0.0 copy-done.7
  7.9 0.2 multiply_reduce_fusion
  8.1 0.0 copy-done.9
  8.1 0.1 copy.101
  8.1 0.1 fusion.66
  8.3 0.1 copy.103
  8.5 0.0 copy-done.10
  8.5 0.5 convolution_convert_fusion.1
  9.0 0.3 broadcast_in_dim.54
  9.2 55.3 %all_to_all.30 = bf16[8,4,16,2048]{3,2,1,0:T(8,128)(2,1)S(1)} all-to-all(bf16[8,4,16,2048]{3,2,1,0:T(8,128)(2,1)S(1)} %bitcast.148), channel_id=1, replica_groups=mesh['wide'=8,'narrow'=4] {'wide'}, dimensions={0} | all-to-all | bytes 4194304 | tf_op jit(solution)/shard_map/all_to_all | solution.py:124
  64.5 1.5 copy.104
  66.1 4.6 %all-to-all-start.1 = ((bf16[8,4,16,2048]{3,2,0,1:T(8,128)(2,1)}), bf16[8,4,16,2048]{3,2,0,1:T(8,128)(2,1)}, u32[]{:S(2)}, u32[]{:S(2)}) async-start(bf16[8,4,16,2048]{3,2,0,1:T(8,128)(2,1)} %copy.104), calls=%async_computation.1 | async-start | bytes 4194304 | tf_op jit(solution)/shard_map/all_to_all | solution.py:123
  70.7 0.0 copy-done.3
  70.7 2.2 copy.106
  72.9 4.3 %copy.125 = f32[48,8,16,128]{3,2,1,0:T(8,128)} copy(f32[48,8,16,128]{3,1,2,0:T(8,128)} %bitcast.146) | data formatting | bytes 6291456
  77.2 2.2 copy.107
  79.4 2.7 %copy.127 = f32[48,8,16,128]{3,2,1,0:T(8,128)S(1)} copy(f32[48,8,16,128]{3,1,2,0:T(8,128)} %bitcast.147) | data formatting | bytes 6291456
  82.2 0.1 copy-done.1
  82.3 1.5 multiply_convert_fusion.1
  83.8 0.3 multiply_convert_fusion
  84.1 12.3 %all-to-all-done.1 = bf16[8,4,16,2048]{3,2,0,1:T(8,128)(2,1)} async-done(((bf16[8,4,16,2048]{3,2,0,1:T(8,128)(2,1)}), bf16[8,4,16,2048]{3,2,0,1:T(8,128)(2,1)}, u32[]{:S(2)}, u32[]{:S(2)}) %all-to-all-start.1) | async-done | bytes 2097184 | tf_op jit(solution)/shard_map/all_to_all | solution.py:123
  96.4 1.8 copy.105
  98.3 0.0 copy-start.2
  98.3 0.2 copy-done.5
  98.5 2.2 fusion.8
  100.6 1.9 mul.168
  102.5 7.2 %convolution_convert_fusion = bf16[512,2048]{1,0:T(8,128)(2,1)} fusion(f32[48,8,16,128]{3,2,1,0:T(8,128)} %bitcast.150, bf16[1,384,2048]{2,1,0:T(8,128)(2,1)} %param.35, bf16[512,2048]{1,0:T(8,128)(2,1)} %bitcast.154, bf16[48,8,16,128]{3,2,1,0:T(8,128)(2,1)S(1)} %bitcast.156, f32[512,384]{1,0:T(8,128)} %fusion.8), kind=kOutput, calls=%fused_computation.5 | convolution fusion | flops 1615200256 | bytes 11272192 | tf_op jit(solution)/shard_map/dot_general | solution.py:34
  109.7 51.8 %all_to_all.31 = bf16[8,4,16,2048]{3,2,1,0:T(8,128)(2,1)S(1)} all-to-all(bf16[8,4,16,2048]{3,2,1,0:T(8,128)(2,1)} %bitcast.155), channel_id=1, replica_groups=mesh['wide'=8,'narrow'=4] {'wide'}, dimensions={0} | all-to-all | bytes 4194304 | tf_op jit(solution)/shard_map/all_to_all | solution.py:136
  161.6 1.4 copy.108
  163.0 4.8 %all-to-all-start.3 = ((bf16[8,4,16,2048]{3,2,0,1:T(8,128)(2,1)}), bf16[8,4,16,2048]{3,2,0,1:T(8,128)(2,1)}, u32[]{:S(2)}, u32[]{:S(2)}) async-start(bf16[8,4,16,2048]{3,2,0,1:T(8,128)(2,1)} %copy.108), calls=%async_computation.3 | async-start | bytes 4194304 | tf_op jit(solution)/shard_map/all_to_all | solution.py:135
  167.8 0.1 copy.102
  167.9 0.1 copy.111
  168.0 0.1 copy.113
  168.1 0.1 copy.112
  168.2 0.0 copy-done.18
  168.3 0.1 select_reduce_fusion
  168.4 25.0 %all-to-all-done.3 = bf16[8,4,16,2048]{3,2,0,1:T(8,128)(2,1)} async-done(((bf16[8,4,16,2048]{3,2,0,1:T(8,128)(2,1)}), bf16[8,4,16,2048]{3,2,0,1:T(8,128)(2,1)}, u32[]{:S(2)}, u32[]{:S(2)}) %all-to-all-start.3) | async-done | bytes 2097184 | tf_op jit(solution)/shard_map/all_to_all | solution.py:135
  193.4 1.7 copy.109
  195.1 0.3 add_bitcast_fusion
  195.5 3.2 %fusion.2 = bf16[16,2048]{1,0:T(8,128)(2,1)S(1)} fusion(f32[16,16,2048]{2,1,0:T(8,128)S(1)} %add_bitcast_fusion, f32[16,16]{0,1:T(8,128)S(1)} %bitcast.166, f32[2,8,16,128]{3,2,1,0:T(8,128)S(1)} %bitcast.160, bf16[16,2048]{1,0:T(8,128)(2,1)S(1)} %copy-done.7, s32[16,16]{0,1:T(8,128)S(1)} %subtract_bitcast_fusion.1, pred[16,16]{0,1:T(8,128)(4,1)S(1)} %get-tuple-element.8), kind=kOutput, calls=%fused_computation.10 | convolution fusion | flops 100806656 | bytes 2361600 | tf_op jit(solution)/shard_map/ecr,ecd->rd/dot_general | solution.py:145
  198.6 0.0 copy-start.8
  198.6 0.0 copy-start.6
  198.7 31.6 %all_gather.3 = bf16[128,2048]{1,0:T(8,128)(2,1)S(1)} all-gather(bf16[16,2048]{1,0:T(8,128)(2,1)S(1)} %fusion.2), channel_id=1, replica_groups=mesh['wide'=8,'narrow'=4] {'wide'}, dimensions={0}, use_global_device_ids=true | all-gather | bytes 589824 | tf_op jit(solution)/shard_map/all_gather | solution.py:149
  230.3 0.6 gather_fusion
  230.9 0.2 fusion.45
  231.1 0.3 convolution_convert_fusion.2
  231.5 8.4 %all_to_all.32 = bf16[4,16,2048]{2,1,0:T(8,128)(2,1)S(1)} all-to-all(bf16[4,16,2048]{2,1,0:T(8,128)(2,1)S(1)} %convolution_convert_fusion.2), channel_id=1, replica_groups=mesh['wide'=8,'narrow'=4] {'narrow'}, dimensions={0} | all-to-all | bytes 524288 | tf_op jit(solution)/shard_map/all_to_all | solution.py:160
  239.9 1.8 fusion.14
  241.7 1.4 convolution_convert_fusion.3
  243.0 3.3 %all-to-all-start.5 = ((bf16[4,16,1024]{2,1,0:T(8,128)(2,1)}), bf16[4,16,1024]{2,1,0:T(8,128)(2,1)S(1)}, u32[]{:S(2)}, u32[]{:S(2)}) async-start(bf16[4,16,1024]{2,1,0:T(8,128)(2,1)} %bitcast.21), calls=%async_computation.5 | async-start | bytes 262144 | tf_op jit(solution)/shard_map/all_to_all | solution.py:165
  246.4 4.6 %all-to-all-done.5 = bf16[4,16,1024]{2,1,0:T(8,128)(2,1)S(1)} async-done(((bf16[4,16,1024]{2,1,0:T(8,128)(2,1)}), bf16[4,16,1024]{2,1,0:T(8,128)(2,1)S(1)}, u32[]{:S(2)}, u32[]{:S(2)}) %all-to-all-start.5) | async-done | bytes 131104 | tf_op jit(solution)/shard_map/all_to_all | solution.py:165
  251.0 1.0 fusion.29
  (44 shorter events, 0.3 us)
Async XLA Ops:
  0.6 241.0 %copy-start = (bf16[1,2048,384]{2,1,0:T(8,128)(2,1)S(1)}, bf16[1,2048,384]{2,1,0:T(8,128)(2,1)}, u32[]{:S(2)}) copy-start(bf16[1,2048,384]{2,1,0:T(8,128)(2,1)} %param.42) | copy-start | bytes 4718596
  3.2 4.7 %copy-start.7 = (bf16[16,2048]{1,0:T(8,128)(2,1)S(1)}, bf16[16,2048]{1,0:T(8,128)(2,1)}, u32[]{:S(2)}) copy-start(bf16[16,2048]{1,0:T(8,128)(2,1)} %param.23) | copy-start | bytes 196612
  3.2 4.8 %copy-start.9 = (s32[16,8]{0,1:T(8,128)S(1)}, s32[16,8]{0,1:T(8,128)}, u32[]{:S(2)}) copy-start(s32[16,8]{0,1:T(8,128)} %param.37) | copy-start | bytes 1540
  5.2 3.3 %copy-start.10 = (bf16[2048]{0:T(1024)(128)(2,1)S(1)}, bf16[2048]{0:T(1024)(128)(2,1)}, u32[]{:S(2)}) copy-start(bf16[2048]{0:T(1024)(128)(2,1)} %param.30) | copy-start | bytes 12292
  66.1 4.6 %copy-start.3 = (bf16[1,2048,384]{2,1,0:T(8,128)(2,1)S(1)}, bf16[1,2048,384]{2,1,0:T(8,128)(2,1)}, u32[]{:S(2)}) copy-start(bf16[1,2048,384]{2,1,0:T(8,128)(2,1)} %param.31) | copy-start | bytes 4718596
  66.1 30.3 %all-to-all-start.1 = ((bf16[8,4,16,2048]{3,2,0,1:T(8,128)(2,1)}), bf16[8,4,16,2048]{3,2,0,1:T(8,128)(2,1)}, u32[]{:S(2)}, u32[]{:S(2)}) async-start(bf16[8,4,16,2048]{3,2,0,1:T(8,128)(2,1)} %copy.104), calls=%async_computation.1 | async-start | bytes 4194304 | tf_op jit(solution)/shard_map/all_to_all | solution.py:123
  72.9 4.3 %copy-start.13 = (f32[1,16,3]{1,0,2:T(1,128)S(1)}, f32[1,16,3]{1,0,2:T(1,128)}, u32[]{:S(2)}) copy-start(f32[1,16,3]{1,0,2:T(1,128)} %param.32) | copy-start | bytes 580
  72.9 4.3 %copy-start.4 = (bf16[1,2048,384]{2,1,0:T(8,128)(2,1)S(1)}, bf16[1,2048,384]{2,1,0:T(8,128)(2,1)}, u32[]{:S(2)}) copy-start(bf16[1,2048,384]{2,1,0:T(8,128)(2,1)} %param.33) | copy-start | bytes 4718596
  79.4 2.7 %copy-start.14 = (f32[1,16,3]{1,0,2:T(1,128)S(1)}, f32[1,16,3]{1,0,2:T(1,128)}, u32[]{:S(2)}) copy-start(f32[1,16,3]{1,0,2:T(1,128)} %param.34) | copy-start | bytes 580
  79.4 2.7 %copy-start.15 = (f32[1,3,16]{2,0,1:T(1,128)S(1)}, f32[1,3,16]{2,0,1:T(1,128)}, u32[]{:S(2)}) copy-start(f32[1,3,16]{2,0,1:T(1,128)} %param.36) | copy-start | bytes 580
  79.4 2.9 %copy-start.1 = (f32[48,8,16,128]{3,2,1,0:T(8,128)S(1)}, f32[48,8,16,128]{3,2,1,0:T(8,128)}, u32[]{:S(2)}) copy-start(f32[48,8,16,128]{3,2,1,0:T(8,128)} %copy.125) | copy-start | bytes 9437188
  96.4 2.0 copy-start.5
  98.3 2.3 copy-start.2
  163.0 4.8 %copy-start.11 = (f32[16,8]{0,1:T(8,128)S(1)}, f32[16,8]{0,1:T(8,128)}, u32[]{:S(2)}) copy-start(f32[16,8]{0,1:T(8,128)} %param.38) | copy-start | bytes 1540
  163.0 4.9 %copy-start.16 = (s32[16,2]{0,1:T(2,128)S(1)}, s32[16,2]{0,1:T(2,128)}, u32[]{:S(2)}) copy-start(s32[16,2]{0,1:T(2,128)} %param.44) | copy-start | bytes 388
  163.0 5.2 %copy-start.12 = (bf16[2048]{0:T(1024)(128)(2,1)S(1)}, bf16[2048]{0:T(1024)(128)(2,1)}, u32[]{:S(2)}) copy-start(bf16[2048]{0:T(1024)(128)(2,1)} %param.40) | copy-start | bytes 12292
  163.0 5.2 %copy-start.18 = (s32[16]{0:T(128)S(1)}, s32[16]{0:T(128)}, u32[]{:S(2)}) copy-start(s32[16]{0:T(128)} %param.39) | copy-start | bytes 196
  163.0 30.3 %all-to-all-start.3 = ((bf16[8,4,16,2048]{3,2,0,1:T(8,128)(2,1)}), bf16[8,4,16,2048]{3,2,0,1:T(8,128)(2,1)}, u32[]{:S(2)}, u32[]{:S(2)}) async-start(bf16[8,4,16,2048]{3,2,0,1:T(8,128)(2,1)} %copy.108), calls=%async_computation.3 | async-start | bytes 4194304 | tf_op jit(solution)/shard_map/all_to_all | solution.py:135
  198.6 44.4 %copy-start.8 = (bf16[16,2048]{1,0:T(8,128)(2,1)}, bf16[16,2048]{1,0:T(8,128)(2,1)S(1)}, u32[]{:S(2)}) copy-start(bf16[16,2048]{1,0:T(8,128)(2,1)S(1)} %fusion.2) | copy-start | bytes 196612
  198.6 43.0 %copy-start.6 = (bf16[1,384,1024]{2,1,0:T(8,128)(2,1)S(1)}, bf16[1,384,1024]{2,1,0:T(8,128)(2,1)}, u32[]{:S(2)}) copy-start(bf16[1,384,1024]{2,1,0:T(8,128)(2,1)} %param.43) | copy-start | bytes 2359300
  239.9 6.5 %copy-start.17 = (f32[16,2]{0,1:T(2,128)S(1)}, f32[16,2]{0,1:T(2,128)}, u32[]{:S(2)}) copy-start(f32[16,2]{0,1:T(2,128)} %param.45) | copy-start | bytes 388
  243.0 7.9 %all-to-all-start.5 = ((bf16[4,16,1024]{2,1,0:T(8,128)(2,1)}), bf16[4,16,1024]{2,1,0:T(8,128)(2,1)S(1)}, u32[]{:S(2)}, u32[]{:S(2)}) async-start(bf16[4,16,1024]{2,1,0:T(8,128)(2,1)} %bitcast.21), calls=%async_computation.5 | async-start | bytes 262144 | tf_op jit(solution)/shard_map/all_to_all | solution.py:165
where the time goes:
time: 253 us; the launch traced here: 252 us
  blocking collectives  147 us (58%)
  waiting for transfers between devices  41.9 us (17%)
  local copies, waits for them, and re-layouts  24.1 us (10%)
  matrix products  21.2 us (8%)
  starting transfers between devices  12.7 us (5%)
  other arithmetic  3.93 us (2%)
    all_to_all x1, blocking collectives, local(): lax.all_to_all(doubled, 'wide', split_axis=0, concat_axis=0, tiled=True)  55.3 us
    all_to_all x1, blocking collectives, local(): lax.all_to_all(produced, 'wide', split_axis=0, concat_axis=0, tiled=True)  51.8 us
    all_gather x1, blocking collectives, local(): gathered = lax.all_gather(thinker_out, 'wide', axis=0, tiled=True)  31.6 us
    all_to_all x1, waiting for transfers between devices, local(): lax.all_to_all(lax.all_to_all(produced, 'wide', split_axis=0, concat_axis...  25 us
    all_to_all x1, waiting for transfers between devices, local(): lax.all_to_all(lax.all_to_all(doubled, 'wide', split_axis=0, concat_axis=...  12.3 us
    dot_general x2, matrix products, swiglu(): jnp.dot(middle, down_dense, preferred_element_type=jnp.float32)  8.55 us
    unnamed x46, local copies, waits for them, and re-layouts  8.53 us
    all_to_all x1, blocking collectives, local(): lax.all_to_all(talk_outgoing, 'narrow', split_axis=0, concat_axis=0, tile...  8.42 us
  transfers between devices with their start and end apart: 3, of which 3 were waited for; matrix products, arithmetic and copies ran while one was open for 5% of the time, Pallas kernels for 0%

commit v1 on v0

--- a/solution.py
+++ b/solution.py
@@ -1,6 +1,8 @@
 import jax
 import jax.numpy as jnp
 from jax import lax
+from jax.experimental import pallas as pl
+from jax.experimental.pallas import tpu as pltpu
 from jax.sharding import PartitionSpec as P
 
 HEADS = 16
@@ -170,9 +172,412 @@
     return (thinker_out, talked.astype(jnp.bfloat16))
 
 
+EXT = 128
+MESH = pl.DeviceIdType.MESH
+
+
+def attention_kernel(
+    hidden_ref, queries_ref, key_ref, value_ref, new_key_ref, new_value_ref, lengths_ref, gain_ref,
+    ids_ref, gates_ref, residual_ref, extended_ref, asked, scores, mixture,
+):
+    rows = hidden_ref.shape[0]
+    breadth = hidden_ref.shape[1]
+    for head in range(HEADS):
+        asked[:, head, :] = queries_ref[:, head * HEAD_DIM : (head + 1) * HEAD_DIM].astype(jnp.float32)
+    scaling = HEAD_DIM ** (-0.5)
+    lower = lax.broadcasted_iota(jnp.int32, (HEADS, HEAD_DIM), 0) < HEADS // KV_HEADS
+    places = lax.broadcasted_iota(jnp.int32, (HEADS, HEAD_DIM), 1)
+    contract = (((1,), (1,)), ((), ()))
+    fresh = []
+    for row in range(rows):
+        query = asked[row]
+        packed = query.astype(jnp.bfloat16)
+        first = lax.dot_general(packed, key_ref[row, :, :HEAD_DIM], contract, preferred_element_type=jnp.float32)
+        second = lax.dot_general(packed, key_ref[row, :, HEAD_DIM:], contract, preferred_element_type=jnp.float32)
+        found = jnp.where(lower, first, second) * scaling
+        scores[row] = jnp.where(places < lengths_ref[row], found, -jnp.inf)
+        newest = jnp.where(
+            lower,
+            new_key_ref[row : row + 1, :HEAD_DIM].astype(jnp.float32),
+            new_key_ref[row : row + 1, HEAD_DIM:].astype(jnp.float32),
+        )
+        fresh.append(jnp.sum(query * newest, axis=1, keepdims=True) * scaling)
+    for row in range(rows):
+        found = scores[row]
+        highest = jnp.maximum(jnp.max(found, axis=1, keepdims=True), fresh[row])
+        weights = jnp.exp(found - highest)
+        own_weight = jnp.exp(fresh[row] - highest)
+        totals = jnp.sum(weights, axis=1, keepdims=True) + own_weight
+        probabilities = (weights / totals).astype(jnp.bfloat16)
+        own_prob = (own_weight / totals).astype(jnp.bfloat16).astype(jnp.float32)
+        first = jnp.dot(probabilities, value_ref[row, :, :HEAD_DIM], preferred_element_type=jnp.float32)
+        second = jnp.dot(probabilities, value_ref[row, :, HEAD_DIM:], preferred_element_type=jnp.float32)
+        newest = jnp.where(
+            lower,
+            new_value_ref[row : row + 1, :HEAD_DIM].astype(jnp.float32),
+            new_value_ref[row : row + 1, HEAD_DIM:].astype(jnp.float32),
+        )
+        mixture[row] = jnp.where(lower, first, second) + own_prob * newest
+    square = jnp.zeros((rows, HEAD_DIM), jnp.float32)
+    for head in range(HEADS):
+        columns = slice(head * HEAD_DIM, (head + 1) * HEAD_DIM)
+        part = hidden_ref[:, columns].astype(jnp.float32) + mixture[:, head, :]
+        residual_ref[:, columns] = part
+        square = square + part * part
+    spread = jnp.sum(square, axis=1, keepdims=True) / breadth
+    factor = lax.rsqrt(spread + EPSILON)
+    extended_ref[:, :breadth] = (residual_ref[...] * factor * gain_ref[...].astype(jnp.float32)).astype(jnp.bfloat16)
+    lanes = lax.broadcasted_iota(jnp.int32, (rows, EXT), 1)
+    named = lanes % 16
+    weight = jnp.zeros((rows, EXT), jnp.float32)
+    for choice in range(TOP):
+        weight = weight + jnp.where(ids_ref[:, choice : choice + 1] == named, gates_ref[:, choice : choice + 1], 0.0)
+    high = weight.astype(jnp.bfloat16).astype(jnp.float32)
+    extended_ref[:, breadth:] = jnp.where(lanes < 16, high, weight - high).astype(jnp.bfloat16)
+
+
+def expert_kernel(
+    residual_ref, extended_ref, gate_scale_ref, up_scale_ref, down_scale_ref, meta_ref, place_ref, talker_gain_ref,
+    gate_hbm, up_hbm, down_hbm, talk_gate_hbm, talk_up_hbm, talk_down_hbm,
+    thinker_ref, talker_ref,
+    gate_w, up_w, down_w, talk_gate_w, talk_up_w, talk_down_w, load_sem,
+    rows_a, rows_b, kept, core_out, core_in, y_out, y_in, x_out, x_in, x_late_out, x_late_in, y_late_out, y_late_in,
+    z_out, z_in, meta_in, meta_rows, talk_rows, spaced, talk_out, talk_in, send_sem, recv_sem,
+):
+    f32, bf16 = jnp.float32, jnp.bfloat16
+    wide, narrow = lax.axis_index("wide"), lax.axis_index("narrow")
+    z, x, y, c = wide // 2, wide % 2, narrow // 2, narrow % 2
+    half = 1024
+
+    def peer(dz, bx, by, bc):
+        there = (z + dz) % 4 if dz else z
+        return (there * 2 + (1 - x if bx else x), (1 - y if by else y) * 2 + (1 - c if bc else c))
+
+    loads = []
+    for number, (source, target) in enumerate((
+        (gate_hbm, gate_w), (up_hbm, up_w), (down_hbm, down_w),
+        (talk_gate_hbm, talk_gate_w), (talk_up_hbm, talk_up_w), (talk_down_hbm, talk_down_w),
+    )):
+        load = pltpu.make_async_copy(source.at[0], target, load_sem.at[number])
+        load.start()
+        loads.append(load)
+    barrier = pltpu.get_barrier_semaphore()
+    everyone = [
+        (dz, bx, by, bc) for dz in range(4) for bx in range(2) for by in range(2) for bc in range(2) if dz or bx or by or bc
+    ]
+    for one in everyone:
+        pl.semaphore_signal(barrier, inc=1, device_id=peer(*one), device_id_type=MESH)
+    rows_a[0, 0, :, :half] = extended_ref[:, :half]
+    rows_a[0, 0, :, half:] = extended_ref[:, 2 * half :]
+    rows_b[0, 0] = extended_ref[:, half : 2 * half]
+    meta_in[0] = meta_ref[0]
+    pl.semaphore_wait(barrier, len(everyone))
+
+    pending = []
+
+    def send(source, target, to):
+        number = len(pending)
+        copy = pltpu.make_async_remote_copy(
+            src_ref=source, dst_ref=target, send_sem=send_sem.at[number], recv_sem=recv_sem.at[number],
+            device_id=peer(*to), device_id_type=MESH,
+        )
+        copy.start()
+        pending.append(copy)
+        return copy
+
+    to_x, to_y, to_c = (0, 1, 0, 0), (0, 0, 1, 0), (0, 0, 0, 1)
+    a_x = [send(rows_a.at[0, 0], rows_a.at[1, 0], to_x)]
+    b_y = [send(rows_b.at[0, 0], rows_b.at[2, 0], to_y)]
+    a_z, b_z = {}, {}
+    for step in (2, 1, 3):
+        a_z[step] = send(rows_a.at[0, 0], rows_a.at[0, 4 - step], (step, 0, 0, 0))
+        b_z[step] = send(rows_b.at[0, 0], rows_b.at[0, 4 - step], (step, 0, 0, 0))
+    a_y = [send(rows_a.at[0, 0], rows_a.at[2, 0], to_y)]
+    b_x = [send(rows_b.at[0, 0], rows_b.at[1, 0], to_x)]
+    meta_copies = []
+    for dz in range(4):
+        for bx in range(2):
+            if dz or bx:
+                meta_copies.append(
+                    send(meta_ref.at[dz * 2 + bx], meta_in.at[(4 - dz) % 4 * 2 + bx], (dz, bx, 0, 0))
+                )
+
+    def scaled(weights, scales, row_block, column_blocks):
+        rows = pl.ds(pl.multiple_of(row_block * BLK, BLK), BLK)
+        for column in range(column_blocks):
+            columns = slice(column * BLK, (column + 1) * BLK)
+            weights[rows, columns] = (weights[rows, columns].astype(f32) * scales[0, row_block, column]).astype(bf16)
+
+    loads[0].wait()
+    loads[1].wait()
+
+    def scale_inner(first, last):
+        def body(row_block, carry):
+            scaled(gate_w, gate_scale_ref, row_block, 3)
+            scaled(up_w, up_scale_ref, row_block, 3)
+            return carry
+
+        lax.fori_loop(first, last, body, 0)
+
+    scale_inner(0, 4)
+    for step in (1, 3, 2):
+        rel = 4 - step
+        a_z[step].wait_recv()
+        a_x.append(send(rows_a.at[0, rel], rows_a.at[1, rel], to_x))
+        b_z[step].wait_recv()
+        b_y.append(send(rows_b.at[0, rel], rows_b.at[2, rel], to_y))
+        a_y.append(send(rows_a.at[0, rel], rows_a.at[2, rel], to_y))
+        b_x.append(send(rows_b.at[0, rel], rows_b.at[1, rel], to_x))
+    across = [send(rows_a.at[0], rows_a.at[4], to_c), send(rows_b.at[0], rows_b.at[4], to_c)]
+    a_far, b_far = [], []
+    for number, rel in enumerate((0, 3, 1, 2)):
+        a_x[number].wait_recv()
+        a_far.append(send(rows_a.at[1, rel], rows_a.at[3, rel], to_y))
+        b_y[number].wait_recv()
+        b_far.append(send(rows_b.at[2, rel], rows_b.at[3, rel], to_x))
+        if number < 3:
+            scale_inner(4 + number * 4, 8 + number * 4)
+    across += [send(rows_a.at[1], rows_a.at[5], to_c), send(rows_b.at[2], rows_b.at[6], to_c)]
+    loads[2].wait()
+
+    def scale_outer(row_block, carry):
+        scaled(down_w, down_scale_ref, row_block, 16)
+        return carry
+
+    lax.fori_loop(0, 3, scale_outer, 0)
+    for copy in a_y + b_x:
+        copy.wait_recv()
+    across += [send(rows_a.at[2], rows_a.at[6], to_c), send(rows_b.at[1], rows_b.at[5], to_c)]
+    for copy in a_far + b_far:
+        copy.wait_recv()
+    across += [send(rows_a.at[3], rows_a.at[7], to_c), send(rows_b.at[3], rows_b.at[7], to_c)]
+
+    def weight_column(extras, first, second):
+        lanes = lax.broadcasted_iota(jnp.int32, extras.shape, 1)
+        return jnp.sum(jnp.where((lanes == first) | (lanes == second), extras.astype(f32), 0.0), axis=1, keepdims=True)
+
+    expert = wide * 2 + narrow // 2
+
+    def hidden_units(base, count):
+        left = rows_a[base : base + count].reshape(count * 64, half + EXT)
+        right = rows_b[base : base + count].reshape(count * 64, half)
+        weight = weight_column(left[:, half:], expert, expert + 16)
+        left = left[:, :half]
+        gated = jnp.dot(left, gate_w[:half], preferred_element_type=f32)
+        gated = gated + jnp.dot(right, gate_w[half:], preferred_element_type=f32)
+        lifted = jnp.dot(left, up_w[:half], preferred_element_type=f32)
+        lifted = lifted + jnp.dot(right, up_w[half:], preferred_element_type=f32)
+        return (jax.nn.silu(gated) * lifted).astype(bf16), weight
+
+    for copy in across:
+        copy.wait_recv()
+    middle, weight = hidden_units(4, 4)
+    for column in range(4):
+        columns = slice(column * 512, (column + 1) * 512)
+        part = jnp.dot(middle, down_w[:, columns], preferred_element_type=f32) * weight
+        core_out[column] = part.astype(bf16)
+    core_copies = [send(core_out.at[column], core_in.at[column], to_c) for column in range(4)]
+    middle, weight = hidden_units(0, 4)
+    for column in range(4):
+        columns = slice(column * 512, (column + 1) * 512)
+        kept[column] = jnp.dot(middle, down_w[:, columns], preferred_element_type=f32) * weight
+    for column in range(4):
+        core_copies[column].wait_recv()
+        kept[column] = kept[column] + core_in[column].astype(f32)
+
+    def piece(group, rel, column):
+        start = group * 64 + rel * 16
+        return kept[column, start : start + 16, :]
+
+    order = (2, 1, 3, 0)
+    first_y, first_x = {}, {}
+    for rel in order:
+        for at in range(2):
+            for column in range(2):
+                span = slice(column * 512, (column + 1) * 512)
+                y_out[rel, at * 16 : (at + 1) * 16, span] = piece(2 + at, rel, column).astype(bf16)
+                x_out[rel, at * 16 : (at + 1) * 16, span] = piece(1 + 2 * at, rel, 2 + column).astype(bf16)
+        first_y[rel] = send(y_out.at[rel], y_in.at[rel], to_y)
+        first_x[rel] = send(x_out.at[rel], x_in.at[rel], to_x)
+    late_x, late_y = {}, {}
+    for rel in order:
+        first_y[rel].wait_recv()
+        first_x[rel].wait_recv()
+        for column in range(2):
+            span = slice(column * 512, (column + 1) * 512)
+            x_late_out[rel, :, span] = (piece(1, rel, column) + y_in[rel, 16:, span].astype(f32)).astype(bf16)
+            y_late_out[rel, :, span] = (piece(2, rel, 2 + column) + x_in[rel, 16:, span].astype(f32)).astype(bf16)
+        late_x[rel] = send(x_late_out.at[rel], x_late_in.at[rel], to_x)
+        late_y[rel] = send(y_late_out.at[rel], y_late_in.at[rel], to_y)
+    own_left = own_right = None
+    z_copies = {}
+    for rel in order:
+        late_x[rel].wait_recv()
+        late_y[rel].wait_recv()
+        sums = []
+        for column in range(4):
+            span = slice(column % 2 * 512, (column % 2 + 1) * 512)
+            early, late = (y_in, x_late_in) if column < 2 else (x_in, y_late_in)
+            sums.append(piece(0, rel, column) + early[rel, :16, span].astype(f32) + late[rel, :, span].astype(f32))
+        if rel:
+            for column in range(4):
+                z_out[rel, :, column * 512 : (column + 1) * 512] = sums[column].astype(bf16)
+            z_copies[rel] = send(z_out.at[rel], z_in.at[4 - rel], (rel, 0, 0, 0))
+    for rel in (1, 2, 3):
+        z_copies[rel].wait_recv()
+    for copy in meta_copies:
+        copy.wait_recv()
+    for load in loads[3:]:
+        load.wait()
+    square = jnp.zeros((16, 512), f32)
+    finals = []
+    for column in range(4):
+        span = slice(column * 512, (column + 1) * 512)
+        total = residual_ref[:, span] + sums[column]
+        for rel in (1, 2, 3):
+            total = total + z_in[rel, :, span].astype(f32)
+        final = total.astype(bf16)
+        thinker_ref[:, span] = final
+        final = final.astype(f32)
+        finals.append(final)
+        square = square + final * final
+    factor = lax.rsqrt(jnp.sum(square, axis=1, keepdims=True) / 2048 + EPSILON)
+    for slot in range(8):
+        meta_rows[2 * slot : 2 * slot + 2, :] = meta_in[slot, 0:2, :]
+    meta = meta_rows[...]
+    picks = (meta[:, 4:5].astype(jnp.int32) == lax.broadcasted_iota(jnp.int32, (16, 16), 1)).astype(f32).astype(bf16)
+    for column in range(4):
+        span = slice(column * 512, (column + 1) * 512)
+        normed = (finals[column] * factor * talker_gain_ref[:, span].astype(f32)).astype(bf16)
+        talk_rows[0, :, span] = jnp.dot(picks, normed, preferred_element_type=f32).astype(bf16)
+    high = meta.astype(bf16).astype(f32)
+    lanes = lax.broadcasted_iota(jnp.int32, meta.shape, 1)
+    talk_rows[0, :, 2048:] = jnp.where(lanes < 8, high, meta - high).astype(bf16)
+    gathers = [send(talk_rows.at[0], talk_rows.at[v], (0, 0, v // 2, v % 2)) for v in (3, 2, 1)]
+    for copy in gathers:
+        copy.wait_recv()
+    inputs = talk_rows[...].reshape(64, 2048 + EXT)
+    weight = weight_column(inputs[:, 2048:], narrow, narrow + 8)
+    inputs = inputs[:, :2048]
+    gated = jnp.dot(inputs, talk_gate_w[...], preferred_element_type=f32)
+    lifted = jnp.dot(inputs, talk_up_w[...], preferred_element_type=f32)
+    middle = (jax.nn.silu(gated) * lifted).astype(bf16)
+    result = jnp.dot(middle, talk_down_w[...], preferred_element_type=f32) * weight
+    for column in range(8):
+        spaced[:, column, :] = result[:, column * 128 : (column + 1) * 128]
+    talk_out[...] = spaced[...].reshape(512, 128).astype(bf16).reshape(4, 8, 16, 128)
+    backs = []
+    for dz in (2, 1, 3, 0):
+        for bx in range(2):
+            for v in range(4):
+                if dz or bx or v:
+                    backs.append(
+                        send(
+                            talk_out.at[v, dz * 2 + bx], talk_in.at[v, (4 - dz) % 4 * 2 + bx], (dz, bx, v // 2, v % 2)
+                        )
+                    )
+    talk_in[0, 0] = talk_out[0, 0]
+    for copy in backs:
+        copy.wait_recv()
+    total = talk_in[0].astype(f32)
+    for v in range(1, 4):
+        total = total + talk_in[v].astype(f32)
+    spaced[:16] = total.reshape(16, 8, 128)
+    for column in range(8):
+        part = spaced[:16, column, :].astype(bf16)
+        talker_ref[:, column * 128 : (column + 1) * 128] = jnp.dot(
+            place_ref[...], part, preferred_element_type=f32
+        ).astype(bf16)
+    for copy in pending:
+        copy.wait_send()
+
+
+def local_fused(
+    hidden_in, queries, cache_key, cache_value, new_key, new_value, lengths, norm_gain, gate_codes, gate_scale,
+    up_codes, up_scale, down_codes, down_scale, think_ids, think_gates, talker_source, talker_gain, talk_gate_w,
+    talk_up_w, talk_down_w, talk_ids, talk_gates,
+):
+    f32, bf16 = jnp.float32, jnp.bfloat16
+    vmem, smem, hbm = (pl.BlockSpec(memory_space=s) for s in (pltpu.VMEM, pltpu.SMEM, pl.ANY))
+    rows, breadth = hidden_in.shape
+    wide = lax.axis_index("wide")
+    residual, extended = pl.pallas_call(
+        attention_kernel,
+        out_shape=(
+            jax.ShapeDtypeStruct((rows, breadth), f32),
+            jax.ShapeDtypeStruct((rows, breadth + EXT), bf16),
+        ),
+        in_specs=[vmem] * 6 + [smem] + [vmem] * 3,
+        out_specs=(vmem, vmem),
+        scratch_shapes=[pltpu.VMEM((rows, HEADS, HEAD_DIM), f32)] * 3,
+        compiler_params=pltpu.CompilerParams(vmem_limit_bytes=24 * 2**20),
+    )(
+        hidden_in, queries, cache_key, cache_value, new_key, new_value, lengths, norm_gain[None, :], think_ids,
+        think_gates,
+    )
+    source_wide = talker_source // (rows * 4)
+    relative = (source_wide // 2 - wide // 2) % 4 * 2 + (source_wide % 2 + wide % 2) % 2
+    same = (relative[:, None] == relative[None, :]) & (jnp.arange(rows)[None, :] < jnp.arange(rows)[:, None])
+    slot = relative * 2 + jnp.sum(same.astype(jnp.int32), axis=1)
+    place = slot[:, None] == jnp.arange(rows)[None, :]
+    weights = jnp.sum(
+        jnp.where(talk_ids[:, :, None] == jnp.arange(4)[None, None, :], talk_gates[:, :, None], 0.0),
+        axis=1,
+    )
+    origin = (talker_source % rows).astype(f32)[:, None]
+    nothing = jnp.zeros((rows, 3), f32)
+    columns = jnp.concatenate([weights, origin, nothing, weights, jnp.zeros((rows, 116), f32)], axis=1)
+    by_slot = jnp.sum(jnp.where(place[:, :, None], columns[:, None, :], 0.0), axis=0)
+    meta = jnp.pad(by_slot.reshape(8, 2, EXT), ((0, 0), (0, 6), (0, 0)))
+    return pl.pallas_call(
+        expert_kernel,
+        out_shape=(jax.ShapeDtypeStruct((rows, breadth), bf16), jax.ShapeDtypeStruct((rows, 1024), bf16)),
+        in_specs=[vmem, vmem, smem, smem, smem, vmem, vmem, vmem] + [hbm] * 6,
+        out_specs=(vmem, vmem),
+        scratch_shapes=[
+            pltpu.VMEM((2048, 384), bf16),
+            pltpu.VMEM((2048, 384), bf16),
+            pltpu.VMEM((384, 2048), bf16),
+            pltpu.VMEM((2048, 384), bf16),
+            pltpu.VMEM((2048, 384), bf16),
+            pltpu.VMEM((384, 1024), bf16),
+            pltpu.SemaphoreType.DMA((6,)),
+            pltpu.VMEM((8, 4, 16, 1024 + EXT), bf16),
+            pltpu.VMEM((8, 4, 16, 1024), bf16),
+            pltpu.VMEM((4, 256, 512), f32),
+            pltpu.VMEM((4, 256, 512), bf16),
+            pltpu.VMEM((4, 256, 512), bf16),
+            pltpu.VMEM((4, 32, 1024), bf16),
+            pltpu.VMEM((4, 32, 1024), bf16),
+            pltpu.VMEM((4, 32, 1024), bf16),
+            pltpu.VMEM((4, 32, 1024), bf16),
+            pltpu.VMEM((4, 16, 1024), bf16),
+            pltpu.VMEM((4, 16, 1024), bf16),
+            pltpu.VMEM((4, 16, 1024), bf16),
+            pltpu.VMEM((4, 16, 1024), bf16),
+            pltpu.VMEM((4, 16, 2048), bf16),
+            pltpu.VMEM((4, 16, 2048), bf16),
+            pltpu.VMEM((8, 8, EXT), f32),
+            pltpu.VMEM((16, EXT), f32),
+            pltpu.VMEM((4, 16, 2048 + EXT), bf16),
+            pltpu.VMEM((64, 8, 128), f32),
+            pltpu.VMEM((4, 8, 16, 128), bf16),
+            pltpu.VMEM((4, 8, 16, 128), bf16),
+            pltpu.SemaphoreType.DMA((112,)),
+            pltpu.SemaphoreType.DMA((112,)),
+        ],
+        compiler_params=pltpu.CompilerParams(
+            collective_id=0, has_side_effects=True, vmem_limit_bytes=44 * 2**20
+        ),
+    )(
+        residual, extended, gate_scale, up_scale, down_scale, meta, place.astype(bf16), talker_gain[None, :],
+        gate_codes, up_codes, down_codes, talk_gate_w, talk_up_w, talk_down_w,
+    )
+
+
 def solution(mesh):
     return jax.shard_map(
-        local,
+        local_fused if mesh.shape["wide"] == 8 and mesh.shape["narrow"] == 4 else local,
         mesh=mesh,
         in_specs=(
             P(("wide", "narrow"), None),

time: 253 us -> 80.6 us (0.32)
  blocking collectives: 147 us -> 0 us
  Pallas kernels: 0 us -> 58.9 us
  waiting for transfers between devices: 41.9 us -> 0 us
  matrix products: 21.2 us -> 0 us
  starting transfers between devices: 12.7 us -> 0 us
  local copies, waits for them, and re-layouts: 24.1 us -> 18.4 us
    all_to_all x3 -> x0, blocking collectives: 116 us -> none  [the longest x1 55.3 us: local(): lax.all_to_all(doubled, 'wide', split_axis=0, concat_axis=0, tiled=True)]
    pallas_call x0 -> x2, Pallas kernels: none -> 58.9 us  [the longest x1 57.3 us: local_fused(): pl.pallas_call(expert_kernel, out_shape=(jax.ShapeDtypeStruct((rows, brea...]
    all_to_all x3 -> x0, waiting for transfers between devices: 41.9 us -> none  [the longest x1 25 us: local(): lax.all_to_all(lax.all_to_all(produced, 'wide', split_axis=0, concat_axis...]
    all_gather x1 -> x0, blocking collectives: 31.6 us -> none  [local(): gathered = lax.all_gather(thinker_out, 'wide', axis=0, tiled=True)]
    dot_general x11 -> x0, matrix products: 21.2 us -> none  [the longest x2 8.55 us: swiglu(): jnp.dot(middle, down_dense, preferred_element_type=jnp.float32)]
    all_to_all x3 -> x0, starting transfers between devices: 12.7 us -> none  [the longest x1 4.76 us: local(): lax.all_to_all(lax.all_to_all(produced, 'wide', split_axis=0, concat_axis...]
    unnamed x46 -> x33, local copies, waits for them, and re-layouts: 8.53 us -> 16.8 us
    all_to_all x4 -> x0, local copies, waits for them, and re-layouts: 6.54 us -> none  [the longest x1 1.85 us: local(): lax.all_to_all(lax.all_to_all(doubled, 'wide', split_axis=0, concat_axis=...]
  transfers between devices with their start and end apart: 3 -> 0, of which waited for: 3 -> 0; matrix products, arithmetic and copies ran while one was open for 5% -> 0% of each run, Pallas kernels for 0% -> 0%
where the time goes in v1:
time: 80.6 us; the launch traced here: 79.9 us
  Pallas kernels  58.9 us (73%)
  local copies, waits for them, and re-layouts  18.4 us (23%)
  other arithmetic  1.87 us (2%)
    pallas_call x1, Pallas kernels, local_fused(): pl.pallas_call(expert_kernel, out_shape=(jax.ShapeDtypeStruct((rows, brea...  57.3 us
    unnamed x33, local copies, waits for them, and re-layouts  16.8 us
    pallas_call x1, Pallas kernels, local_fused(): pl.pallas_call(attention_kernel, out_shape=(jax.ShapeDtypeStruct((rows, b...  1.62 us

profile of v1, /device:TPU:0, one launch (start us, length us, event | category | flops | bytes accessed | tf_op | source)
XLA Modules:
  0.0 79.9 jit_solution(6363647248698165916)
XLA Ops:
  0.6 0.0 copy-start
  0.7 0.8 fusion.1
  1.5 0.2 convert_reduce_fusion
  1.6 0.7 copy.40.down_scale_ref
  2.3 0.7 select_reduce_fusion.1
  3.0 0.1 fusion.8
  3.1 0.1 copy.35
  3.2 0.1 copy.36
  3.3 0.7 broadcast_in_dim.58.gain_ref
  4.0 0.8 copy.38.gate_scale_ref
  4.7 0.8 copy.39.up_scale_ref
  5.5 0.8 copy.33.ids_ref
  6.2 0.8 copy.34.gates_ref
  7.0 0.7 broadcast_in_dim.67.talker_gain_ref
  7.7 0.1 concatenate.3
  7.8 0.1 select_reduce_fusion
  7.9 0.0 copy-start.5
  7.9 1.2 %copy-done.5 = bf16[16,128,256]{2,1,0:T(8,128)(2,1)S(1)} copy-done((bf16[16,128,256]{2,1,0:T(8,128)(2,1)S(1)}, bf16[16,128,256]{2,1,0:T(8,128)(2,1)}, u32[]{:S(2)}) %copy-start.5) | copy-done | bytes 1048600
  9.1 0.0 copy-start.6
  9.1 1.2 %copy-done.6 = bf16[16,128,256]{2,1,0:T(8,128)(2,1)S(1)} copy-done((bf16[16,128,256]{2,1,0:T(8,128)(2,1)S(1)}, bf16[16,128,256]{2,1,0:T(8,128)(2,1)}, u32[]{:S(2)}) %copy-start.6) | copy-done | bytes 1048600
  10.4 0.0 copy-start.8
  10.4 0.8 %copy-done.8 = bf16[16,2048]{1,0:T(8,128)(2,1)S(1)} copy-done((bf16[16,2048]{1,0:T(8,128)(2,1)S(1)}, bf16[16,2048]{1,0:T(8,128)(2,1)}, u32[]{:S(2)}) %copy-start.8) | copy-done | bytes 65560
  11.2 0.0 copy-start.9
  11.2 0.8 %copy-done.9 = bf16[16,2048]{1,0:T(8,128)(2,1)S(1)} copy-done((bf16[16,2048]{1,0:T(8,128)(2,1)S(1)}, bf16[16,2048]{1,0:T(8,128)(2,1)}, u32[]{:S(2)}) %copy-start.9) | copy-done | bytes 65560
  12.0 0.0 copy-start.10
  12.0 0.7 copy-done.10
  12.7 0.0 copy-start.11
  12.7 0.7 copy-done.11
  13.4 0.0 copy-start.12
  13.4 0.7 copy-done.12
  14.1 0.0 copy-start.7
  14.1 1.6 %shard_map.230 = (f32[16,2048]{1,0:T(8,128)S(1)}, bf16[16,2176]{1,0:T(8,128)(2,1)S(1)}) custom-call(bf16[16,2048]{1,0:T(8,128)(2,1)S(1)} %copy-done.8, bf16[16,2048]{1,0:T(8,128)(2,1)S(1)} %copy-done.9, bf16[16,128,256]{2,1,0:T(8,128)(2,1)S(1)} %copy-done.5, bf16[16,128,256]{2,1,0:T(8,128)(2,1)S(1)} %copy-done.6, bf16[16,256]{1,0:T(8,128)(2,1)S(1)} %copy-done.10, ...), custom_call_target="tpu_custom_call" | custom-call | tf_op jit(solution)/shard_map/pallas_call | solution.py:504
  15.7 0.0 copy-done
  15.7 0.0 copy-done.7
  15.7 0.0 copy-start.1
  15.8 1.4 %copy-done.1 = bf16[1,2048,384]{2,1,0:T(8,128)(2,1)S(1)} copy-done((bf16[1,2048,384]{2,1,0:T(8,128)(2,1)S(1)}, bf16[1,2048,384]{2,1,0:T(8,128)(2,1)}, u32[]{:S(2)}) %copy-start.1) | copy-done | bytes 1572888
  17.2 0.0 copy-start.2
  17.2 1.4 %copy-done.2 = bf16[1,384,2048]{2,1,0:T(8,128)(2,1)S(1)} copy-done((bf16[1,384,2048]{2,1,0:T(8,128)(2,1)S(1)}, bf16[1,384,2048]{2,1,0:T(8,128)(2,1)}, u32[]{:S(2)}) %copy-start.2) | copy-done | bytes 1572888
  18.6 0.0 copy-start.3
  18.6 1.4 %copy-done.3 = bf16[1,2048,384]{2,1,0:T(8,128)(2,1)S(1)} copy-done((bf16[1,2048,384]{2,1,0:T(8,128)(2,1)S(1)}, bf16[1,2048,384]{2,1,0:T(8,128)(2,1)}, u32[]{:S(2)}) %copy-start.3) | copy-done | bytes 1572888
  20.0 0.0 copy-start.4
  20.0 1.4 %copy-done.4 = bf16[1,2048,384]{2,1,0:T(8,128)(2,1)S(1)} copy-done((bf16[1,2048,384]{2,1,0:T(8,128)(2,1)S(1)}, bf16[1,2048,384]{2,1,0:T(8,128)(2,1)}, u32[]{:S(2)}) %copy-start.4) | copy-done | bytes 1572888
  21.4 57.3 %shard_map.231 = (bf16[16,2048]{1,0:T(8,128)(2,1)S(1)}, bf16[16,1024]{1,0:T(8,128)(2,1)S(1)}) custom-call(f32[16,2048]{1,0:T(8,128)S(1)} %get-tuple-element.4.residual_ref, bf16[16,2176]{1,0:T(8,128)(2,1)S(1)} %get-tuple-element.5.extended_ref, f32[1,16,3]{2,1,0:T(8,128)S(1)} %copy.38.gate_scale_ref, f32[1,16,3]{2,1,0:T(8,128)S(1)} %copy.39.up_scale_ref, ...), custom_call_target="tpu_custom_call" | custom-call | tf_op jit(solution)/shard_map/pallas_call | solution.py:532
  78.6 0.6 copy.43
  79.3 0.6 copy.44
  (4 shorter events, 0.0 us)
Async XLA Ops:
  0.6 15.1 %copy-start = (bf16[1,2048,384]{2,1,0:T(8,128)(2,1)S(1)}, bf16[1,2048,384]{2,1,0:T(8,128)(2,1)}, u32[]{:S(2)}) copy-start(bf16[1,2048,384]{2,1,0:T(8,128)(2,1)} %gate_hbm.1) | copy-start | bytes 4718596
  7.9 1.2 %copy-start.5 = (bf16[16,128,256]{2,1,0:T(8,128)(2,1)S(1)}, bf16[16,128,256]{2,1,0:T(8,128)(2,1)}, u32[]{:S(2)}) copy-start(bf16[16,128,256]{2,1,0:T(8,128)(2,1)} %key_ref.1) | copy-start | bytes 3145732
  9.1 1.2 %copy-start.6 = (bf16[16,128,256]{2,1,0:T(8,128)(2,1)S(1)}, bf16[16,128,256]{2,1,0:T(8,128)(2,1)}, u32[]{:S(2)}) copy-start(bf16[16,128,256]{2,1,0:T(8,128)(2,1)} %value_ref.1) | copy-start | bytes 3145732
  10.4 0.8 %copy-start.8 = (bf16[16,2048]{1,0:T(8,128)(2,1)S(1)}, bf16[16,2048]{1,0:T(8,128)(2,1)}, u32[]{:S(2)}) copy-start(bf16[16,2048]{1,0:T(8,128)(2,1)} %hidden_ref.1) | copy-start | bytes 196612
  11.2 0.8 %copy-start.9 = (bf16[16,2048]{1,0:T(8,128)(2,1)S(1)}, bf16[16,2048]{1,0:T(8,128)(2,1)}, u32[]{:S(2)}) copy-start(bf16[16,2048]{1,0:T(8,128)(2,1)} %queries_ref.1) | copy-start | bytes 196612
  12.0 0.7 copy-start.10
  12.7 0.7 copy-start.11
  13.4 0.7 copy-start.12
  14.1 1.6 %copy-start.7 = (bf16[1,384,1024]{2,1,0:T(8,128)(2,1)S(1)}, bf16[1,384,1024]{2,1,0:T(8,128)(2,1)}, u32[]{:S(2)}) copy-start(bf16[1,384,1024]{2,1,0:T(8,128)(2,1)} %talk_down_hbm.1) | copy-start | bytes 2359300
  15.7 1.4 %copy-start.1 = (bf16[1,2048,384]{2,1,0:T(8,128)(2,1)S(1)}, bf16[1,2048,384]{2,1,0:T(8,128)(2,1)}, u32[]{:S(2)}) copy-start(bf16[1,2048,384]{2,1,0:T(8,128)(2,1)} %up_hbm.1) | copy-start | bytes 4718596
  17.2 1.4 %copy-start.2 = (bf16[1,384,2048]{2,1,0:T(8,128)(2,1)S(1)}, bf16[1,384,2048]{2,1,0:T(8,128)(2,1)}, u32[]{:S(2)}) copy-start(bf16[1,384,2048]{2,1,0:T(8,128)(2,1)} %down_hbm.1) | copy-start | bytes 4718596
  18.6 1.4 %copy-start.3 = (bf16[1,2048,384]{2,1,0:T(8,128)(2,1)S(1)}, bf16[1,2048,384]{2,1,0:T(8,128)(2,1)}, u32[]{:S(2)}) copy-start(bf16[1,2048,384]{2,1,0:T(8,128)(2,1)} %talk_gate_hbm.1) | copy-start | bytes 4718596
  20.0 1.4 %copy-start.4 = (bf16[1,2048,384]{2,1,0:T(8,128)(2,1)S(1)}, bf16[1,2048,384]{2,1,0:T(8,128)(2,1)}, u32[]{:S(2)}) copy-start(bf16[1,2048,384]{2,1,0:T(8,128)(2,1)} %talk_up_hbm.1) | copy-start | bytes 4718596

commit v2 on v1

--- a/solution.py
+++ b/solution.py
@@ -176,14 +176,12 @@
 MESH = pl.DeviceIdType.MESH
 
 
-def attention_kernel(
-    hidden_ref, queries_ref, key_ref, value_ref, new_key_ref, new_value_ref, lengths_ref, gain_ref,
-    ids_ref, gates_ref, residual_ref, extended_ref, asked, scores, mixture,
+def attention(
+    hidden, queries, keys, values, new_key, new_value, lengths_ref, gain, asked, scores, mixture, residual, before_values
 ):
-    rows = hidden_ref.shape[0]
-    breadth = hidden_ref.shape[1]
+    rows, breadth = residual.shape
     for head in range(HEADS):
-        asked[:, head, :] = queries_ref[:, head * HEAD_DIM : (head + 1) * HEAD_DIM].astype(jnp.float32)
+        asked[:, head, :] = queries[:, head * HEAD_DIM : (head + 1) * HEAD_DIM].astype(jnp.float32)
     scaling = HEAD_DIM ** (-0.5)
     lower = lax.broadcasted_iota(jnp.int32, (HEADS, HEAD_DIM), 0) < HEADS // KV_HEADS
     places = lax.broadcasted_iota(jnp.int32, (HEADS, HEAD_DIM), 1)
@@ -192,16 +190,17 @@
     for row in range(rows):
         query = asked[row]
         packed = query.astype(jnp.bfloat16)
-        first = lax.dot_general(packed, key_ref[row, :, :HEAD_DIM], contract, preferred_element_type=jnp.float32)
-        second = lax.dot_general(packed, key_ref[row, :, HEAD_DIM:], contract, preferred_element_type=jnp.float32)
+        first = lax.dot_general(packed, keys[row, :, :HEAD_DIM], contract, preferred_element_type=jnp.float32)
+        second = lax.dot_general(packed, keys[row, :, HEAD_DIM:], contract, preferred_element_type=jnp.float32)
         found = jnp.where(lower, first, second) * scaling
         scores[row] = jnp.where(places < lengths_ref[row], found, -jnp.inf)
         newest = jnp.where(
             lower,
-            new_key_ref[row : row + 1, :HEAD_DIM].astype(jnp.float32),
-            new_key_ref[row : row + 1, HEAD_DIM:].astype(jnp.float32),
+            new_key[row : row + 1, :HEAD_DIM].astype(jnp.float32),
+            new_key[row : row + 1, HEAD_DIM:].astype(jnp.float32),
         )
         fresh.append(jnp.sum(query * newest, axis=1, keepdims=True) * scaling)
+    before_values()
     for row in range(rows):
         found = scores[row]
         highest = jnp.maximum(jnp.max(found, axis=1, keepdims=True), fresh[row])
@@ -210,39 +209,37 @@
         totals = jnp.sum(weights, axis=1, keepdims=True) + own_weight
         probabilities = (weights / totals).astype(jnp.bfloat16)
         own_prob = (own_weight / totals).astype(jnp.bfloat16).astype(jnp.float32)
-        first = jnp.dot(probabilities, value_ref[row, :, :HEAD_DIM], preferred_element_type=jnp.float32)
-        second = jnp.dot(probabilities, value_ref[row, :, HEAD_DIM:], preferred_element_type=jnp.float32)
+        first = jnp.dot(probabilities, values[row, :, :HEAD_DIM], preferred_element_type=jnp.float32)
+        second = jnp.dot(probabilities, values[row, :, HEAD_DIM:], preferred_element_type=jnp.float32)
         newest = jnp.where(
             lower,
-            new_value_ref[row : row + 1, :HEAD_DIM].astype(jnp.float32),
-            new_value_ref[row : row + 1, HEAD_DIM:].astype(jnp.float32),
+            new_value[row : row + 1, :HEAD_DIM].astype(jnp.float32),
+            new_value[row : row + 1, HEAD_DIM:].astype(jnp.float32),
         )
         mixture[row] = jnp.where(lower, first, second) + own_prob * newest
     square = jnp.zeros((rows, HEAD_DIM), jnp.float32)
     for head in range(HEADS):
         columns = slice(head * HEAD_DIM, (head + 1) * HEAD_DIM)
-        part = hidden_ref[:, columns].astype(jnp.float32) + mixture[:, head, :]
-        residual_ref[:, columns] = part
+        part = hidden[:, columns].astype(jnp.float32) + mixture[:, head, :]
+        residual[:, columns] = part
         square = square + part * part
-    spread = jnp.sum(square, axis=1, keepdims=True) / breadth
-    factor = lax.rsqrt(spread + EPSILON)
-    extended_ref[:, :breadth] = (residual_ref[...] * factor * gain_ref[...].astype(jnp.float32)).astype(jnp.bfloat16)
-    lanes = lax.broadcasted_iota(jnp.int32, (rows, EXT), 1)
-    named = lanes % 16
-    weight = jnp.zeros((rows, EXT), jnp.float32)
-    for choice in range(TOP):
-        weight = weight + jnp.where(ids_ref[:, choice : choice + 1] == named, gates_ref[:, choice : choice + 1], 0.0)
-    high = weight.astype(jnp.bfloat16).astype(jnp.float32)
-    extended_ref[:, breadth:] = jnp.where(lanes < 16, high, weight - high).astype(jnp.bfloat16)
-
-
-def expert_kernel(
-    residual_ref, extended_ref, gate_scale_ref, up_scale_ref, down_scale_ref, meta_ref, place_ref, talker_gain_ref,
-    gate_hbm, up_hbm, down_hbm, talk_gate_hbm, talk_up_hbm, talk_down_hbm,
+    factor = lax.rsqrt(jnp.sum(square, axis=1, keepdims=True) / breadth + EPSILON)
+    normed = []
+    for head in range(HEADS):
+        part = residual[:, head * HEAD_DIM : (head + 1) * HEAD_DIM] * factor
+        normed.append((part * gain[head : head + 1, :].astype(jnp.float32)).astype(jnp.bfloat16))
+    return normed
+
+
+def layer_kernel(
+    lengths_ref, source_ref, gate_scale_ref, up_scale_ref, down_scale_ref, key_hbm, queries_hbm, new_key_hbm, value_hbm,
+    new_value_hbm, hidden_hbm, gain_hbm, ids_hbm, gates_hbm, talk_ids_hbm, talk_gates_hbm, gate_hbm, up_hbm, down_hbm,
+    talker_gain_hbm, talk_gate_hbm, talk_up_hbm, talk_down_hbm,
     thinker_ref, talker_ref,
-    gate_w, up_w, down_w, talk_gate_w, talk_up_w, talk_down_w, load_sem,
+    keys, queries, new_key, values, new_value, hidden, gain, ids, gates, talk_ids, talk_gates, gate_w, up_w, down_w,
+    talker_gain, talk_gate_w, talk_up_w, talk_down_w, load_sem, asked, scores, mixture, residual,
     rows_a, rows_b, kept, core_out, core_in, y_out, y_in, x_out, x_in, x_late_out, x_late_in, y_late_out, y_late_in,
-    z_out, z_in, meta_in, meta_rows, talk_rows, spaced, talk_out, talk_in, send_sem, recv_sem,
+    z_out, z_in, meta_out, meta_in, meta_rows, talk_rows, spaced, talk_out, talk_in, send_sem, recv_sem,
 ):
     f32, bf16 = jnp.float32, jnp.bfloat16
     wide, narrow = lax.axis_index("wide"), lax.axis_index("narrow")
@@ -255,10 +252,13 @@
 
     loads = []
     for number, (source, target) in enumerate((
-        (gate_hbm, gate_w), (up_hbm, up_w), (down_hbm, down_w),
-        (talk_gate_hbm, talk_gate_w), (talk_up_hbm, talk_up_w), (talk_down_hbm, talk_down_w),
+        (key_hbm, keys), (queries_hbm, queries), (new_key_hbm, new_key), (value_hbm, values),
+        (new_value_hbm, new_value), (hidden_hbm, hidden), (gain_hbm, gain), (ids_hbm, ids), (gates_hbm, gates),
+        (talk_ids_hbm, talk_ids), (talk_gates_hbm, talk_gates), (gate_hbm.at[0], gate_w), (up_hbm.at[0], up_w),
+        (down_hbm.at[0], down_w), (talker_gain_hbm, talker_gain), (talk_gate_hbm.at[0], talk_gate_w),
+        (talk_up_hbm.at[0], talk_up_w), (talk_down_hbm.at[0], talk_down_w),
     )):
-        load = pltpu.make_async_copy(source.at[0], target, load_sem.at[number])
+        load = pltpu.make_async_copy(source, target, load_sem.at[number])
         load.start()
         loads.append(load)
     barrier = pltpu.get_barrier_semaphore()
@@ -267,10 +267,66 @@
     ]
     for one in everyone:
         pl.semaphore_signal(barrier, inc=1, device_id=peer(*one), device_id_type=MESH)
-    rows_a[0, 0, :, :half] = extended_ref[:, :half]
-    rows_a[0, 0, :, half:] = extended_ref[:, 2 * half :]
-    rows_b[0, 0] = extended_ref[:, half : 2 * half]
-    meta_in[0] = meta_ref[0]
+
+    down_iota = lax.broadcasted_iota(jnp.int32, (16, 16), 0)
+    along_iota = lax.broadcasted_iota(jnp.int32, (16, 16), 1)
+    rel_down, rel_along, origin = (jnp.zeros((16, 16), jnp.int32) for _ in range(3))
+    for position in range(16):
+        number = source_ref[position]
+        from_wide = lax.div(number, 64)
+        from_z, from_x = lax.div(from_wide, 2), lax.rem(from_wide, 2)
+        relative = lax.rem(from_z - z + 4, 4) * 2 + lax.rem(from_x + x, 2)
+        rel_down = jnp.where(down_iota == position, relative, rel_down)
+        rel_along = jnp.where(along_iota == position, relative, rel_along)
+        origin = jnp.where(along_iota == position, lax.rem(number, 16), origin)
+    same = rel_down == rel_along
+    rank_down = jnp.sum(jnp.where(same & (along_iota < down_iota), 1.0, 0.0), axis=1, keepdims=True)
+    rank_along = jnp.sum(jnp.where(same & (down_iota < along_iota), 1.0, 0.0), axis=0, keepdims=True)
+    slot_down = rel_down.astype(f32) * 2 + rank_down
+    slot_along = rel_along.astype(f32) * 2 + rank_along
+    place = jnp.where(slot_down == along_iota.astype(f32), 1.0, 0.0).astype(bf16)
+    place_across = jnp.where(slot_along == down_iota.astype(f32), 1.0, 0.0).astype(bf16)
+    identity = jnp.where(down_iota == along_iota, 1.0, 0.0).astype(bf16)
+    contract = (((1,), (1,)), ((), ()))
+    lines = lax.broadcasted_iota(jnp.int32, (EXT, 16), 0)
+    for number in range(7, 11):
+        loads[number].wait()
+    weight = jnp.zeros((EXT, 16), f32)
+    for choice in range(TOP):
+        weight = weight + jnp.where(ids[choice : choice + 1, :] == lines % 16, gates[choice : choice + 1, :], 0.0)
+    high = weight.astype(bf16).astype(f32)
+    split = jnp.where(lines < 16, high, weight - high).astype(bf16)
+    extras = lax.dot_general(identity, split, contract, preferred_element_type=f32).astype(bf16)
+    weight = jnp.zeros((EXT, 16), f32)
+    for choice in range(TTOP):
+        weight = weight + jnp.where(
+            talk_ids[choice : choice + 1, :] == lines % 8, talk_gates[choice : choice + 1, :], 0.0
+        )
+    high = weight.astype(bf16).astype(f32)
+    split = jnp.where(lines < 8, high, weight - high)
+    split = jnp.where(lines == 4, origin[0:1, :].astype(f32), split).astype(bf16)
+    by_slot = lax.dot_general(place_across, split, contract, preferred_element_type=f32)
+    meta_out[...] = jnp.zeros_like(meta_out)
+    for slot in range(8):
+        meta_out[slot, 0:2, :] = by_slot[2 * slot : 2 * slot + 2, :]
+    meta_in[0] = meta_out[0]
+
+    for number in range(3):
+        loads[number].wait()
+
+    def before_values():
+        for number in range(3, 7):
+            loads[number].wait()
+
+    normed = attention(
+        hidden, queries, keys, values, new_key, new_value, lengths_ref, gain, asked, scores, mixture, residual,
+        before_values,
+    )
+    for head in range(8):
+        columns = slice(head * HEAD_DIM, (head + 1) * HEAD_DIM)
+        rows_a[0, 0, :, columns] = normed[head]
+        rows_b[0, 0, :, columns] = normed[8 + head]
+    rows_a[0, 0, :, half:] = extras
     pl.semaphore_wait(barrier, len(everyone))
 
     pending = []
@@ -286,35 +342,35 @@
         return copy
 
     to_x, to_y, to_c = (0, 1, 0, 0), (0, 0, 1, 0), (0, 0, 0, 1)
-    a_x = [send(rows_a.at[0, 0], rows_a.at[1, 0], to_x)]
-    b_y = [send(rows_b.at[0, 0], rows_b.at[2, 0], to_y)]
+    a_x = [send(rows_a.at[0, 0], rows_a.at[2, 0], to_x)]
+    b_y = [send(rows_b.at[0, 0], rows_b.at[4, 0], to_y)]
     a_z, b_z = {}, {}
     for step in (2, 1, 3):
         a_z[step] = send(rows_a.at[0, 0], rows_a.at[0, 4 - step], (step, 0, 0, 0))
         b_z[step] = send(rows_b.at[0, 0], rows_b.at[0, 4 - step], (step, 0, 0, 0))
-    a_y = [send(rows_a.at[0, 0], rows_a.at[2, 0], to_y)]
-    b_x = [send(rows_b.at[0, 0], rows_b.at[1, 0], to_x)]
+    a_y = [send(rows_a.at[0, 0], rows_a.at[4, 0], to_y)]
+    b_x = [send(rows_b.at[0, 0], rows_b.at[2, 0], to_x)]
     meta_copies = []
     for dz in range(4):
         for bx in range(2):
             if dz or bx:
                 meta_copies.append(
-                    send(meta_ref.at[dz * 2 + bx], meta_in.at[(4 - dz) % 4 * 2 + bx], (dz, bx, 0, 0))
+                    send(meta_out.at[dz * 2 + bx], meta_in.at[(4 - dz) % 4 * 2 + bx], (dz, bx, 0, 0))
                 )
 
-    def scaled(weights, scales, row_block, column_blocks):
+    def scaled(weights, scale, row_block, column_blocks):
         rows = pl.ds(pl.multiple_of(row_block * BLK, BLK), BLK)
         for column in range(column_blocks):
             columns = slice(column * BLK, (column + 1) * BLK)
-            weights[rows, columns] = (weights[rows, columns].astype(f32) * scales[0, row_block, column]).astype(bf16)
-
-    loads[0].wait()
-    loads[1].wait()
+            weights[rows, columns] = (weights[rows, columns].astype(f32) * scale(row_block, column)).astype(bf16)
+
+    loads[11].wait()
+    loads[12].wait()
 
     def scale_inner(first, last):
         def body(row_block, carry):
-            scaled(gate_w, gate_scale_ref, row_block, 3)
-            scaled(up_w, up_scale_ref, row_block, 3)
+            scaled(gate_w, lambda i, j: gate_scale_ref[j, 0, i], row_block, 3)
+            scaled(up_w, lambda i, j: up_scale_ref[j, 0, i], row_block, 3)
             return carry
 
         lax.fori_loop(first, last, body, 0)
@@ -323,42 +379,36 @@
     for step in (1, 3, 2):
         rel = 4 - step
         a_z[step].wait_recv()
-        a_x.append(send(rows_a.at[0, rel], rows_a.at[1, rel], to_x))
+        a_x.append(send(rows_a.at[0, rel], rows_a.at[2, rel], to_x))
         b_z[step].wait_recv()
-        b_y.append(send(rows_b.at[0, rel], rows_b.at[2, rel], to_y))
-        a_y.append(send(rows_a.at[0, rel], rows_a.at[2, rel], to_y))
-        b_x.append(send(rows_b.at[0, rel], rows_b.at[1, rel], to_x))
-    across = [send(rows_a.at[0], rows_a.at[4], to_c), send(rows_b.at[0], rows_b.at[4], to_c)]
+        b_y.append(send(rows_b.at[0, rel], rows_b.at[4, rel], to_y))
+        a_y.append(send(rows_a.at[0, rel], rows_a.at[4, rel], to_y))
+        b_x.append(send(rows_b.at[0, rel], rows_b.at[2, rel], to_x))
+    across = [send(rows_a.at[0], rows_a.at[1], to_c), send(rows_b.at[0], rows_b.at[1], to_c)]
     a_far, b_far = [], []
     for number, rel in enumerate((0, 3, 1, 2)):
         a_x[number].wait_recv()
-        a_far.append(send(rows_a.at[1, rel], rows_a.at[3, rel], to_y))
+        a_far.append(send(rows_a.at[2, rel], rows_a.at[6, rel], to_y))
         b_y[number].wait_recv()
-        b_far.append(send(rows_b.at[2, rel], rows_b.at[3, rel], to_x))
+        b_far.append(send(rows_b.at[4, rel], rows_b.at[6, rel], to_x))
         if number < 3:
             scale_inner(4 + number * 4, 8 + number * 4)
-    across += [send(rows_a.at[1], rows_a.at[5], to_c), send(rows_b.at[2], rows_b.at[6], to_c)]
-    loads[2].wait()
+    across += [send(rows_a.at[2], rows_a.at[3], to_c), send(rows_b.at[4], rows_b.at[5], to_c)]
+    loads[13].wait()
 
     def scale_outer(row_block, carry):
-        scaled(down_w, down_scale_ref, row_block, 16)
+        scaled(down_w, lambda i, j: down_scale_ref[i, 0, j], row_block, 16)
         return carry
 
     lax.fori_loop(0, 3, scale_outer, 0)
-    for copy in a_y + b_x:
-        copy.wait_recv()
-    across += [send(rows_a.at[2], rows_a.at[6], to_c), send(rows_b.at[1], rows_b.at[5], to_c)]
-    for copy in a_far + b_far:
-        copy.wait_recv()
-    across += [send(rows_a.at[3], rows_a.at[7], to_c), send(rows_b.at[3], rows_b.at[7], to_c)]
-
     def weight_column(extras, first, second):
         lanes = lax.broadcasted_iota(jnp.int32, extras.shape, 1)
         return jnp.sum(jnp.where((lanes == first) | (lanes == second), extras.astype(f32), 0.0), axis=1, keepdims=True)
 
     expert = wide * 2 + narrow // 2
 
-    def hidden_units(base, count):
+    def hidden_units(first, count):
+        base, count = 2 * first, 2 * count
         left = rows_a[base : base + count].reshape(count * 64, half + EXT)
         right = rows_b[base : base + count].reshape(count * 64, half)
         weight = weight_column(left[:, half:], expert, expert + 16)
@@ -369,71 +419,84 @@
         lifted = lifted + jnp.dot(right, up_w[half:], preferred_element_type=f32)
         return (jax.nn.silu(gated) * lifted).astype(bf16), weight
 
-    for copy in across:
-        copy.wait_recv()
-    middle, weight = hidden_units(4, 4)
-    for column in range(4):
-        columns = slice(column * 512, (column + 1) * 512)
-        part = jnp.dot(middle, down_w[:, columns], preferred_element_type=f32) * weight
-        core_out[column] = part.astype(bf16)
-    core_copies = [send(core_out.at[column], core_in.at[column], to_c) for column in range(4)]
-    middle, weight = hidden_units(0, 4)
-    for column in range(4):
-        columns = slice(column * 512, (column + 1) * 512)
-        kept[column] = jnp.dot(middle, down_w[:, columns], preferred_element_type=f32) * weight
-    for column in range(4):
-        core_copies[column].wait_recv()
-        kept[column] = kept[column] + core_in[column].astype(f32)
-
-    def piece(group, rel, column):
-        start = group * 64 + rel * 16
-        return kept[column, start : start + 16, :]
-
+    core_copies = {}
+
+    def process(first, count):
+        middle, weight = hidden_units(first, count)
+        for column in range(4):
+            columns = slice(column * 512, (column + 1) * 512)
+            part = jnp.dot(middle, down_w[:, columns], preferred_element_type=f32) * weight
+            for at in range(count):
+                kept[first + at, :, columns] = part[at * 128 : at * 128 + 64]
+                core_out[first + at, :, columns] = part[at * 128 + 64 : at * 128 + 128].astype(bf16)
+        for group in range(first, first + count):
+            core_copies[group] = send(core_out.at[group], core_in.at[group], to_c)
+
+    across[0].wait_recv()
+    across[1].wait_recv()
+    process(0, 1)
+    for copy in a_y + b_x:
+        copy.wait_recv()
+    across += [send(rows_a.at[4], rows_a.at[5], to_c), send(rows_b.at[2], rows_b.at[3], to_c)]
+    for copy in across[2:]:
+        copy.wait_recv()
+    process(1, 2)
+    for copy in a_far + b_far:
+        copy.wait_recv()
+    across_far = [send(rows_a.at[6], rows_a.at[7], to_c), send(rows_b.at[6], rows_b.at[7], to_c)]
+    for group in range(3):
+        core_copies[group].wait_recv()
+        kept[group] = kept[group] + core_in[group].astype(f32)
+    for rel in range(4):
+        y_out[0, rel] = kept[2, rel * 16 : (rel + 1) * 16, :half].astype(bf16)
+        x_out[0, rel] = kept[1, rel * 16 : (rel + 1) * 16, half:].astype(bf16)
+    near = [send(y_out.at[0], y_in.at[0], to_y), send(x_out.at[0], x_in.at[0], to_x)]
+    for copy in across_far:
+        copy.wait_recv()
+    process(3, 1)
+    core_copies[3].wait_recv()
     order = (2, 1, 3, 0)
     first_y, first_x = {}, {}
     for rel in order:
-        for at in range(2):
-            for column in range(2):
-                span = slice(column * 512, (column + 1) * 512)
-                y_out[rel, at * 16 : (at + 1) * 16, span] = piece(2 + at, rel, column).astype(bf16)
-                x_out[rel, at * 16 : (at + 1) * 16, span] = piece(1 + 2 * at, rel, 2 + column).astype(bf16)
-        first_y[rel] = send(y_out.at[rel], y_in.at[rel], to_y)
-        first_x[rel] = send(x_out.at[rel], x_in.at[rel], to_x)
+        span = slice(rel * 16, (rel + 1) * 16)
+        y_out[1, rel] = (kept[3, span, :half] + core_in[3, span, :half].astype(f32)).astype(bf16)
+        x_out[1, rel] = (kept[3, span, half:] + core_in[3, span, half:].astype(f32)).astype(bf16)
+        first_y[rel] = send(y_out.at[1, rel], y_in.at[1, rel], to_y)
+        first_x[rel] = send(x_out.at[1, rel], x_in.at[1, rel], to_x)
     late_x, late_y = {}, {}
     for rel in order:
+        span = slice(rel * 16, (rel + 1) * 16)
         first_y[rel].wait_recv()
+        x_late_out[rel] = (kept[1, span, :half] + y_in[1, rel].astype(f32)).astype(bf16)
+        late_x[rel] = send(x_late_out.at[rel], x_late_in.at[rel], to_x)
         first_x[rel].wait_recv()
-        for column in range(2):
-            span = slice(column * 512, (column + 1) * 512)
-            x_late_out[rel, :, span] = (piece(1, rel, column) + y_in[rel, 16:, span].astype(f32)).astype(bf16)
-            y_late_out[rel, :, span] = (piece(2, rel, 2 + column) + x_in[rel, 16:, span].astype(f32)).astype(bf16)
-        late_x[rel] = send(x_late_out.at[rel], x_late_in.at[rel], to_x)
+        y_late_out[rel] = (kept[2, span, half:] + x_in[1, rel].astype(f32)).astype(bf16)
         late_y[rel] = send(y_late_out.at[rel], y_late_in.at[rel], to_y)
-    own_left = own_right = None
+    for copy in near:
+        copy.wait_recv()
     z_copies = {}
     for rel in order:
+        span = slice(rel * 16, (rel + 1) * 16)
         late_x[rel].wait_recv()
         late_y[rel].wait_recv()
-        sums = []
-        for column in range(4):
-            span = slice(column % 2 * 512, (column % 2 + 1) * 512)
-            early, late = (y_in, x_late_in) if column < 2 else (x_in, y_late_in)
-            sums.append(piece(0, rel, column) + early[rel, :16, span].astype(f32) + late[rel, :, span].astype(f32))
+        left = kept[0, span, :half] + y_in[0, rel].astype(f32) + x_late_in[rel].astype(f32)
+        right = kept[0, span, half:] + x_in[0, rel].astype(f32) + y_late_in[rel].astype(f32)
         if rel:
-            for column in range(4):
-                z_out[rel, :, column * 512 : (column + 1) * 512] = sums[column].astype(bf16)
+            z_out[rel, :, :half] = left.astype(bf16)
+            z_out[rel, :, half:] = right.astype(bf16)
             z_copies[rel] = send(z_out.at[rel], z_in.at[4 - rel], (rel, 0, 0, 0))
+    sums = [left[:, :512], left[:, 512:], right[:, :512], right[:, 512:]]
     for rel in (1, 2, 3):
         z_copies[rel].wait_recv()
     for copy in meta_copies:
         copy.wait_recv()
-    for load in loads[3:]:
+    for load in loads[14:]:
         load.wait()
     square = jnp.zeros((16, 512), f32)
     finals = []
     for column in range(4):
         span = slice(column * 512, (column + 1) * 512)
-        total = residual_ref[:, span] + sums[column]
+        total = residual[:, span] + sums[column]
         for rel in (1, 2, 3):
             total = total + z_in[rel, :, span].astype(f32)
         final = total.astype(bf16)
@@ -448,11 +511,12 @@
     picks = (meta[:, 4:5].astype(jnp.int32) == lax.broadcasted_iota(jnp.int32, (16, 16), 1)).astype(f32).astype(bf16)
     for column in range(4):
         span = slice(column * 512, (column + 1) * 512)
-        normed = (finals[column] * factor * talker_gain_ref[:, span].astype(f32)).astype(bf16)
-        talk_rows[0, :, span] = jnp.dot(picks, normed, preferred_element_type=f32).astype(bf16)
-    high = meta.astype(bf16).astype(f32)
-    lanes = lax.broadcasted_iota(jnp.int32, meta.shape, 1)
-    talk_rows[0, :, 2048:] = jnp.where(lanes < 8, high, meta - high).astype(bf16)
+        for block in range(4):
+            row = column * 4 + block
+            normed = finals[column][:, block * BLK : (block + 1) * BLK] * factor
+            normed = (normed * talker_gain[row : row + 1, :].astype(f32)).astype(bf16)
+            talk_rows[0, :, row * BLK : (row + 1) * BLK] = jnp.dot(picks, normed, preferred_element_type=f32).astype(bf16)
+    talk_rows[0, :, 2048:] = meta.astype(bf16)
     gathers = [send(talk_rows.at[0], talk_rows.at[v], (0, 0, v // 2, v % 2)) for v in (3, 2, 1)]
     for copy in gathers:
         copy.wait_recv()
@@ -486,7 +550,7 @@
     for column in range(8):
         part = spaced[:16, column, :].astype(bf16)
         talker_ref[:, column * 128 : (column + 1) * 128] = jnp.dot(
-            place_ref[...], part, preferred_element_type=f32
+            place, part, preferred_element_type=f32
         ).astype(bf16)
     for copy in pending:
         copy.wait_send()
@@ -498,65 +562,46 @@
     talk_up_w, talk_down_w, talk_ids, talk_gates,
 ):
     f32, bf16 = jnp.float32, jnp.bfloat16
-    vmem, smem, hbm = (pl.BlockSpec(memory_space=s) for s in (pltpu.VMEM, pltpu.SMEM, pl.ANY))
+    vmem, smem, hbm = (pl.BlockSpec(memory_space=s) for s in (pltpu.VMEM, pltpu.SMEM, pltpu.HBM))
+    operands = [
+        lengths, talker_source, jnp.transpose(gate_scale, (2, 0, 1)), jnp.transpose(up_scale, (2, 0, 1)),
+        jnp.transpose(down_scale, (1, 0, 2)), cache_key, queries, new_key, cache_value, new_value, hidden_in,
+        norm_gain.reshape(16, 128), think_ids.T, think_gates.T, talk_ids.T, talk_gates.T, gate_codes, up_codes,
+        down_codes, talker_gain.reshape(16, 128), talk_gate_w, talk_up_w, talk_down_w,
+    ]
+    landing = []
+    for operand in operands[5:]:
+        shape = operand.shape[1:] if operand.shape[0] == 1 else operand.shape
+        landing.append(pltpu.VMEM(shape, operand.dtype))
     rows, breadth = hidden_in.shape
-    wide = lax.axis_index("wide")
-    residual, extended = pl.pallas_call(
-        attention_kernel,
-        out_shape=(
-            jax.ShapeDtypeStruct((rows, breadth), f32),
-            jax.ShapeDtypeStruct((rows, breadth + EXT), bf16),
-        ),
-        in_specs=[vmem] * 6 + [smem] + [vmem] * 3,
+    return pl.pallas_call(
+        layer_kernel,
+        out_shape=(jax.ShapeDtypeStruct((rows, breadth), bf16), jax.ShapeDtypeStruct((rows, 1024), bf16)),
+        in_specs=[smem] * 5 + [hbm] * 18,
         out_specs=(vmem, vmem),
-        scratch_shapes=[pltpu.VMEM((rows, HEADS, HEAD_DIM), f32)] * 3,
-        compiler_params=pltpu.CompilerParams(vmem_limit_bytes=24 * 2**20),
-    )(
-        hidden_in, queries, cache_key, cache_value, new_key, new_value, lengths, norm_gain[None, :], think_ids,
-        think_gates,
-    )
-    source_wide = talker_source // (rows * 4)
-    relative = (source_wide // 2 - wide // 2) % 4 * 2 + (source_wide % 2 + wide % 2) % 2
-    same = (relative[:, None] == relative[None, :]) & (jnp.arange(rows)[None, :] < jnp.arange(rows)[:, None])
-    slot = relative * 2 + jnp.sum(same.astype(jnp.int32), axis=1)
-    place = slot[:, None] == jnp.arange(rows)[None, :]
-    weights = jnp.sum(
-        jnp.where(talk_ids[:, :, None] == jnp.arange(4)[None, None, :], talk_gates[:, :, None], 0.0),
-        axis=1,
-    )
-    origin = (talker_source % rows).astype(f32)[:, None]
-    nothing = jnp.zeros((rows, 3), f32)
-    columns = jnp.concatenate([weights, origin, nothing, weights, jnp.zeros((rows, 116), f32)], axis=1)
-    by_slot = jnp.sum(jnp.where(place[:, :, None], columns[:, None, :], 0.0), axis=0)
-    meta = jnp.pad(by_slot.reshape(8, 2, EXT), ((0, 0), (0, 6), (0, 0)))
-    return pl.pallas_call(
-        expert_kernel,
-        out_shape=(jax.ShapeDtypeStruct((rows, breadth), bf16), jax.ShapeDtypeStruct((rows, 1024), bf16)),
-        in_specs=[vmem, vmem, smem, smem, smem, vmem, vmem, vmem] + [hbm] * 6,
-        out_specs=(vmem, vmem),
-        scratch_shapes=[
-            pltpu.VMEM((2048, 384), bf16),
-            pltpu.VMEM((2048, 384), bf16),
-            pltpu.VMEM((384, 2048), bf16),
-            pltpu.VMEM((2048, 384), bf16),
-            pltpu.VMEM((2048, 384), bf16),
-            pltpu.VMEM((384, 1024), bf16),
-            pltpu.SemaphoreType.DMA((6,)),
+        scratch_shapes=landing
+        + [
+            pltpu.SemaphoreType.DMA((18,)),
+            pltpu.VMEM((rows, HEADS, HEAD_DIM), f32),
+            pltpu.VMEM((rows, HEADS, HEAD_DIM), f32),
+            pltpu.VMEM((rows, HEADS, HEAD_DIM), f32),
+            pltpu.VMEM((rows, breadth), f32),
             pltpu.VMEM((8, 4, 16, 1024 + EXT), bf16),
             pltpu.VMEM((8, 4, 16, 1024), bf16),
-            pltpu.VMEM((4, 256, 512), f32),
-            pltpu.VMEM((4, 256, 512), bf16),
-            pltpu.VMEM((4, 256, 512), bf16),
-            pltpu.VMEM((4, 32, 1024), bf16),
-            pltpu.VMEM((4, 32, 1024), bf16),
-            pltpu.VMEM((4, 32, 1024), bf16),
-            pltpu.VMEM((4, 32, 1024), bf16),
+            pltpu.VMEM((4, 64, 2048), f32),
+            pltpu.VMEM((4, 64, 2048), bf16),
+            pltpu.VMEM((4, 64, 2048), bf16),
+            pltpu.VMEM((2, 4, 16, 1024), bf16),
+            pltpu.VMEM((2, 4, 16, 1024), bf16),
+            pltpu.VMEM((2, 4, 16, 1024), bf16),
+            pltpu.VMEM((2, 4, 16, 1024), bf16),
             pltpu.VMEM((4, 16, 1024), bf16),
             pltpu.VMEM((4, 16, 1024), bf16),
             pltpu.VMEM((4, 16, 1024), bf16),
             pltpu.VMEM((4, 16, 1024), bf16),
             pltpu.VMEM((4, 16, 2048), bf16),
             pltpu.VMEM((4, 16, 2048), bf16),
+            pltpu.VMEM((8, 8, EXT), f32),
             pltpu.VMEM((8, 8, EXT), f32),
             pltpu.VMEM((16, EXT), f32),
             pltpu.VMEM((4, 16, 2048 + EXT), bf16),
@@ -567,12 +612,9 @@
             pltpu.SemaphoreType.DMA((112,)),
         ],
         compiler_params=pltpu.CompilerParams(
-            collective_id=0, has_side_effects=True, vmem_limit_bytes=44 * 2**20
+            collective_id=0, has_side_effects=True, vmem_limit_bytes=48 * 2**20
         ),
-    )(
-        residual, extended, gate_scale, up_scale, down_scale, meta, place.astype(bf16), talker_gain[None, :],
-        gate_codes, up_codes, down_codes, talk_gate_w, talk_up_w, talk_down_w,
-    )
+    )(*operands)
 
 
 def solution(mesh):

time: 80.6 us -> 74.8 us (0.928)
  Pallas kernels: 58.9 us -> 56.7 us
  other arithmetic: 1.87 us -> 0 us
  local copies, waits for them, and re-layouts: 18.4 us -> 16.8 us
    pallas_call x2 -> x1, Pallas kernels: 58.9 us -> 56.7 us  [local_fused(): pl.pallas_call(layer_kernel, out_shape=(jax.ShapeDtypeStruct((rows, bread...]
    broadcast_in_dim x5 -> x0, local copies, waits for them, and re-layouts: 1.47 us -> none  [the longest x1 0.69 us: local_fused(): norm_gain[None, :]]
    reduce_sum x3 -> x0, other arithmetic: 1 us -> none  [the longest x1 0.71 us: local_fused(): jnp.sum(jnp.where(talk_ids[:, :, None] == jnp.arange(4)[None, None, :], t...]
    unnamed x33 -> x40, local copies, waits for them, and re-layouts: 16.8 us -> 16.8 us
where the time goes in v2:
time: 74.8 us; the launch traced here: 74.1 us
  Pallas kernels  56.7 us (76%)
  local copies, waits for them, and re-layouts  16.8 us (22%)
    pallas_call x1, Pallas kernels, local_fused(): pl.pallas_call(layer_kernel, out_shape=(jax.ShapeDtypeStruct((rows, bread...  56.7 us
    unnamed x40, local copies, waits for them, and re-layouts  16.8 us

profile of v2, /device:TPU:0, one launch (start us, length us, event | category | flops | bytes accessed | tf_op | source)
XLA Modules:
  0.0 74.1 jit_solution(9081840225016221475)
XLA Ops:
  0.6 0.0 copy-start
  0.6 1.4 %copy-done = bf16[1,2048,384]{2,1,0:T(8,128)(2,1)S(1)} copy-done((bf16[1,2048,384]{2,1,0:T(8,128)(2,1)S(1)}, bf16[1,2048,384]{2,1,0:T(8,128)(2,1)}, u32[]{:S(2)}) %copy-start) | copy-done | bytes 1572888
  2.0 0.0 copy-start.1
  2.0 1.2 %copy-done.1 = bf16[16,128,256]{2,1,0:T(8,128)(2,1)S(1)} copy-done((bf16[16,128,256]{2,1,0:T(8,128)(2,1)S(1)}, bf16[16,128,256]{2,1,0:T(8,128)(2,1)}, u32[]{:S(2)}) %copy-start.1) | copy-done | bytes 1048600
  3.3 0.0 copy-start.2
  3.3 1.2 %copy-done.2 = bf16[16,128,256]{2,1,0:T(8,128)(2,1)S(1)} copy-done((bf16[16,128,256]{2,1,0:T(8,128)(2,1)S(1)}, bf16[16,128,256]{2,1,0:T(8,128)(2,1)}, u32[]{:S(2)}) %copy-start.2) | copy-done | bytes 1048600
  4.5 0.0 copy-start.3
  4.5 1.1 %copy-done.3 = bf16[1,384,1024]{2,1,0:T(8,128)(2,1)S(1)} copy-done((bf16[1,384,1024]{2,1,0:T(8,128)(2,1)S(1)}, bf16[1,384,1024]{2,1,0:T(8,128)(2,1)}, u32[]{:S(2)}) %copy-start.3) | copy-done | bytes 786456
  5.6 0.0 copy-start.4
  5.6 0.8 %copy-done.4 = bf16[16,2048]{1,0:T(8,128)(2,1)S(1)} copy-done((bf16[16,2048]{1,0:T(8,128)(2,1)S(1)}, bf16[16,2048]{1,0:T(8,128)(2,1)}, u32[]{:S(2)}) %copy-start.4) | copy-done | bytes 65560
  6.5 0.0 copy-start.5
  6.5 0.8 %copy-done.5 = bf16[16,2048]{1,0:T(8,128)(2,1)S(1)} copy-done((bf16[16,2048]{1,0:T(8,128)(2,1)S(1)}, bf16[16,2048]{1,0:T(8,128)(2,1)}, u32[]{:S(2)}) %copy-start.5) | copy-done | bytes 65560
  7.3 0.0 copy-start.6
  7.3 0.7 copy-done.6
  8.0 0.0 copy-start.7
  8.0 0.7 copy-done.7
  8.7 0.0 copy-start.8
  8.7 0.7 copy-done.8
  9.4 0.0 copy-start.9
  9.4 0.7 copy-done.9
  10.1 0.0 copy-start.10
  10.1 0.7 copy-done.10
  10.8 0.0 copy-start.11
  10.8 0.7 copy-done.11
  11.5 0.0 copy-start.12
  11.5 0.7 copy-done.12
  12.1 0.0 copy-start.13
  12.1 0.7 copy-done.13
  12.8 0.0 copy-start.14
  12.8 0.7 copy-done.14
  13.5 0.0 copy-start.15
  13.5 0.7 copy-done.15
  14.2 0.0 copy-start.16
  14.2 0.7 copy-done.16
  14.9 0.0 copy-start.17
  14.9 0.7 copy-done.17
  15.5 0.0 copy-start.18
  15.5 0.7 copy-done.18
  16.2 56.7 %shard_map.230 = (bf16[16,2048]{1,0:T(8,128)(2,1)S(1)}, bf16[16,1024]{1,0:T(8,128)(2,1)S(1)}) custom-call(s32[16]{0:T(128)S(1)} %copy-done.17, s32[16]{0:T(128)S(1)} %copy-done.18, f32[3,1,16]{2,1,0:T(1,128)S(1)} %bitcast.13, f32[3,1,16]{2,1,0:T(1,128)S(1)} %bitcast.14, f32[3,1,16]{2,1,0:T(1,128)S(1)} %bitcast.15, bf16[16,128,256]{2,1,0:T(8,128)(2,1)S(1)} %copy-done.1, ...), custom_call_target="tpu_custom_call" | custom-call | tf_op jit(solution)/shard_map/pallas_call | solution.py:577
  72.9 0.6 copy.27
  73.5 0.6 copy.28
Async XLA Ops:
  0.6 1.4 %copy-start = (bf16[1,2048,384]{2,1,0:T(8,128)(2,1)S(1)}, bf16[1,2048,384]{2,1,0:T(8,128)(2,1)}, u32[]{:S(2)}) copy-start(bf16[1,2048,384]{2,1,0:T(8,128)(2,1)} %gate_hbm.1) | copy-start | bytes 4718596
  2.0 1.2 %copy-start.1 = (bf16[16,128,256]{2,1,0:T(8,128)(2,1)S(1)}, bf16[16,128,256]{2,1,0:T(8,128)(2,1)}, u32[]{:S(2)}) copy-start(bf16[16,128,256]{2,1,0:T(8,128)(2,1)} %key_hbm.1) | copy-start | bytes 3145732
  3.3 1.2 %copy-start.2 = (bf16[16,128,256]{2,1,0:T(8,128)(2,1)S(1)}, bf16[16,128,256]{2,1,0:T(8,128)(2,1)}, u32[]{:S(2)}) copy-start(bf16[16,128,256]{2,1,0:T(8,128)(2,1)} %value_hbm.1) | copy-start | bytes 3145732
  4.5 1.1 %copy-start.3 = (bf16[1,384,1024]{2,1,0:T(8,128)(2,1)S(1)}, bf16[1,384,1024]{2,1,0:T(8,128)(2,1)}, u32[]{:S(2)}) copy-start(bf16[1,384,1024]{2,1,0:T(8,128)(2,1)} %talk_down_hbm.1) | copy-start | bytes 2359300
  5.6 0.8 %copy-start.4 = (bf16[16,2048]{1,0:T(8,128)(2,1)S(1)}, bf16[16,2048]{1,0:T(8,128)(2,1)}, u32[]{:S(2)}) copy-start(bf16[16,2048]{1,0:T(8,128)(2,1)} %queries_hbm.1) | copy-start | bytes 196612
  6.5 0.8 %copy-start.5 = (bf16[16,2048]{1,0:T(8,128)(2,1)S(1)}, bf16[16,2048]{1,0:T(8,128)(2,1)}, u32[]{:S(2)}) copy-start(bf16[16,2048]{1,0:T(8,128)(2,1)} %hidden_hbm.1) | copy-start | bytes 196612
  7.3 0.7 copy-start.6
  8.0 0.7 copy-start.7
  8.7 0.7 copy-start.8
  9.4 0.7 copy-start.9
  10.1 0.7 copy-start.10
  10.8 0.7 copy-start.11
  11.5 0.7 copy-start.12
  12.1 0.7 copy-start.13
  12.8 0.7 copy-start.14
  13.5 0.7 copy-start.15
  14.2 0.7 copy-start.16
  14.9 0.7 copy-start.17
  15.5 0.7 copy-start.18

commit v3 on v2

--- a/solution.py
+++ b/solution.py
@@ -612,7 +612,7 @@
             pltpu.SemaphoreType.DMA((112,)),
         ],
         compiler_params=pltpu.CompilerParams(
-            collective_id=0, has_side_effects=True, vmem_limit_bytes=48 * 2**20
+            collective_id=0, has_side_effects=True, vmem_limit_bytes=60 * 2**20
         ),
     )(*operands)
 

time: 74.8 us -> 61.3 us (0.82)
  local copies, waits for them, and re-layouts: 16.8 us -> 2.85 us
  Pallas kernels: 56.7 us -> 57.5 us
    unnamed x40 -> x2, local copies, waits for them, and re-layouts: 16.8 us -> 2.85 us
    pallas_call x1, Pallas kernels: 56.7 us -> 57.5 us  [local_fused(): pl.pallas_call(layer_kernel, out_shape=(jax.ShapeDtypeStruct((rows, bread...]
where the time goes in v3:
time: 61.3 us; the launch traced here: 61 us
  Pallas kernels  57.5 us (94%)
  local copies, waits for them, and re-layouts  2.85 us (5%)
  between operations  0.65 us (1%)
    pallas_call x1, Pallas kernels, local_fused(): pl.pallas_call(layer_kernel, out_shape=(jax.ShapeDtypeStruct((rows, bread...  57.5 us
    unnamed x2, local copies, waits for them, and re-layouts  2.85 us

profile of v3, /device:TPU:0, one launch (start us, length us, event | category | flops | bytes accessed | tf_op | source)
XLA Modules:
  0.0 61.0 jit_solution(15778824416558874072)
XLA Ops:
  0.6 57.5 %shard_map.230 = (bf16[16,2048]{1,0:T(8,128)(2,1)}, bf16[16,1024]{1,0:T(8,128)(2,1)}) custom-call(s32[16]{0:T(128)} %lengths_ref.1, s32[16]{0:T(128)} %source_ref.1, f32[3,1,16]{2,1,0:T(1,128)} %bitcast.13, f32[3,1,16]{2,1,0:T(1,128)} %bitcast.14, f32[3,1,16]{2,1,0:T(1,128)} %bitcast.15, bf16[16,128,256]{2,1,0:T(8,128)(2,1)} %key_hbm.1, ...), custom_call_target="tpu_custom_call" | custom-call | tf_op jit(solution)/shard_map/pallas_call | solution.py:577
  58.2 1.5 %copy.27 = bf16[16,2048]{1,0:T(8,128)(2,1)} copy(bf16[16,2048]{1,0:T(8,128)(2,1)} %get-tuple-element.4) | data formatting | bytes 131072
  59.7 1.4 %copy.28 = bf16[16,1024]{1,0:T(8,128)(2,1)} copy(bf16[16,1024]{1,0:T(8,128)(2,1)} %get-tuple-element.5) | data formatting | bytes 65536
